TPU v7x, 32 devices: a whole 2x2x4 slice. The times are simulated.
32 devices in a mesh: rep: 16 (over z, y, core), grp: 2 (over x).
Axes of the slice: x: 2, y: 2, z: 4, core: 2. Of those that a mesh axis runs over, the one named last changes fastest.
Arguments:
- inputs: bfloat16 [32, 1024, 768], P('rep', 'grp'), may hold values from -6 to 6
- pre_gain: bfloat16 [768], P('grp'), may hold values from 0.25 to 1.75
- w_in: bfloat16 [768, 3328], P('grp'), may hold values from -0.21875 to 0.21875
- w_dt: bfloat16 [768, 24], P('grp'), may hold values from -0.21875 to 0.21875
- conv_w: bfloat16 [4, 1792], P(None, 'grp'), may hold values from -3 to 3
- conv_b: bfloat16 [1792], P('grp'), may hold values from -4 to 4
- dt_bias: bfloat16 [24], P('grp'), may hold values from -4.5 to -3.5
- a_log: bfloat16 [24], P('grp'), as said below
- d_skip: bfloat16 [24], P('grp'), may hold values from 0.5 to 1.5
- norm_gain: bfloat16 [1536], P('grp'), may hold values from 0.25 to 1.75
- w_out: bfloat16 [1536, 768], P('grp'), may hold values from -0.15625 to 0.15625
- cotangent: bfloat16 [32, 1024, 768], P('rep', 'grp'), may hold values from -6 to 6
Outputs:
- output: bfloat16 [32, 1024, 768], P('rep', 'grp')
- d_input: bfloat16 [32, 1024, 768], P('rep', 'grp')
- grad_pre_gain: float32 [768], P('grp')
- grad_w_in: float32 [768, 3328], P('grp')
- grad_w_dt: float32 [768, 24], P('grp')
- grad_conv_w: float32 [4, 1792], P(None, 'grp')
- grad_conv_b: float32 [1792], P('grp')
- grad_dt_bias: float32 [24], P('grp')
- grad_a_log: float32 [24], P('grp')
- grad_d_skip: float32 [24], P('grp')
- grad_norm_gain: float32 [1536], P('grp')
- grad_w_out: float32 [1536, 768], P('grp')
Inputs may be any that keep to these rules, and one draw needn't show every extreme that they name: `a_log`: each head's log-rate, independent over heads.
All inputs are finite; a program needn't handle non-finite values.
Results may differ from a plain program's by a relative error of at most 0.0075.
Values may be sent and summed in bfloat16 or wider, within the bound.
A program may use at most 192 MiB of HBM per device.

v0:
```python
import jax
import jax.numpy as jnp
from jax import lax
from jax.sharding import PartitionSpec as P

E = 1536
H = 24
P_SIZE = 64
N = 128
K = 4
BLOCK = 256


exact_mode = lax.Precision.HIGHEST


def passed_along(shard, axis, by):
    size = lax.axis_size(axis)
    pairs = [(i, i + by) for i in range(size) if 0 <= i + by < size]
    return lax.ppermute(shard, axis, pairs)


def prefix_2(value, axis, join, neutral, backward):
    count, mine = (lax.axis_size(axis), lax.axis_index(axis))
    pieces = jax.tree.map(lambda part: lax.all_gather(part, axis), value)
    if backward:
        pieces = jax.tree.map(lambda part: part[::-1], pieces)
        mine = count - 1 - mine
    running = jax.tree.map(
        lambda part, zero: jnp.full_like(part, 0) + jnp.asarray(zero, part.dtype), value, neutral
    )

    def step(position, running):
        longer = join(running, jax.tree.map(lambda part: part[position], pieces))
        return jax.tree.map(lambda new, old: jnp.where(position < mine, new, old), longer, running)

    return lax.fori_loop(0, count - 1, step, running)


def rms_scale(values, gain_vector):
    return (
        values * lax.rsqrt(jnp.mean(values * values, axis=-1, keepdims=True) + 1e-05) * gain_vector
    )


def mix_inputs(xbc_piece, rim_rows, dt_linear, conv_weight, conv_bias, bias_dt, log_rate):
    extended = jnp.concatenate([rim_rows, xbc_piece], axis=1)
    length = xbc_piece.shape[1]
    summed = jnp.zeros_like(xbc_piece) + conv_bias
    for offset in range(K):
        summed = summed + conv_weight[offset] * extended[:, offset : offset + length, :]
    mixed_rows = jax.nn.silu(summed)
    blocks = xbc_piece.shape[0] * (length // BLOCK)
    heads_x = mixed_rows[..., :E].reshape(blocks, BLOCK, H, P_SIZE)
    b_rows = mixed_rows[..., E : E + N].reshape(blocks, BLOCK, N)
    c_rows = mixed_rows[..., E + N :].reshape(blocks, BLOCK, N)
    step_size = jax.nn.softplus(dt_linear + bias_dt).reshape(blocks, BLOCK, H)
    decay_rate = -step_size * jnp.exp(log_rate)
    return (heads_x, b_rows, c_rows, step_size, decay_rate)


def block_stats(heads_x, b_rows, step_size, decay_rate):
    cumul = jnp.cumsum(decay_rate, axis=1)
    weights_last = jnp.exp(cumul[:, -1:, :] - cumul) * step_size
    states = jnp.einsum(
        "mqhp,mqn->mhpn", weights_last[..., None] * heads_x, b_rows, precision=exact_mode
    )
    return (states, jnp.exp(cumul[:, -1, :]))


def block_out(operands):
    heads_x, b_rows, c_rows, step_size, decay_rate, start_state = operands
    cumul = jnp.cumsum(decay_rate, axis=0)
    places = jnp.arange(BLOCK)
    lower_mask = (places[:, None] >= places[None, :]).astype(jnp.float32)
    spread = cumul.T[:, :, None] - cumul.T[:, None, :]
    decays = jnp.exp(spread * lower_mask) * lower_mask
    scores = jnp.dot(c_rows, b_rows.T, precision=exact_mode)
    mixing = scores[None] * decays * step_size.T[:, None, :]
    inner_part = jnp.einsum("hts,shp->thp", mixing, heads_x, precision=exact_mode)
    carried = jnp.einsum("tn,hpn->thp", c_rows, start_state, precision=exact_mode)
    return inner_part + carried * jnp.exp(cumul)[:, :, None]


def mixer_out(
    heads_x, b_rows, c_rows, step_size, decay_rate, starts, skip_gain, gate_rows, gain_norm
):
    outputs = lax.map(
        jax.checkpoint(block_out), (heads_x, b_rows, c_rows, step_size, decay_rate, starts)
    )
    mixed_y = outputs + skip_gain[:, None] * heads_x
    gated_rows = mixed_y.reshape(gate_rows.shape) * jax.nn.silu(gate_rows)
    return rms_scale(gated_rows, gain_norm)


def chain_forward(states, decays):

    def stepper(running, operands):
        state_add, decay_now = operands
        return (decay_now[..., None, None] * running + state_add, running)

    final_state, local_starts = lax.scan(
        stepper,
        jnp.zeros_like(states[:, 0]),
        (jnp.moveaxis(states, 1, 0), jnp.moveaxis(decays, 1, 0)),
    )
    return (jnp.moveaxis(local_starts, 0, 1), final_state)


def chain_back(gradients, decays):

    def stepper(running, operands):
        grad_now, decay_now = operands
        return (grad_now + decay_now[..., None, None] * running, running)

    first_local, after_local = lax.scan(
        stepper,
        jnp.zeros_like(gradients[:, 0]),
        (jnp.moveaxis(gradients, 1, 0), jnp.moveaxis(decays, 1, 0)),
        reverse=True,
    )
    return (jnp.moveaxis(after_local, 0, 1), first_local)


def join_states(earlier, later):
    return (earlier[0] * later[0], later[0][..., None, None] * earlier[1] + later[1])


def per_device(
    inputs,
    pre_gain,
    w_in,
    w_dt,
    conv_w,
    conv_b,
    dt_bias,
    a_log,
    d_skip,
    norm_gain,
    w_out,
    cotangent,
):
    seq_count, piece_len, model_width = inputs.shape
    tok_rows = seq_count * piece_len
    rim_len = K - 1
    per_seq = piece_len // BLOCK
    gathered = (
        lax.all_gather(pre_gain, "grp", axis=0, tiled=True),
        lax.all_gather(w_in, "grp", axis=0, tiled=True),
        lax.all_gather(w_dt, "grp", axis=0, tiled=True),
        lax.all_gather(conv_w, "grp", axis=1, tiled=True),
        lax.all_gather(conv_b, "grp", axis=0, tiled=True),
        lax.all_gather(dt_bias, "grp", axis=0, tiled=True),
        lax.all_gather(a_log, "grp", axis=0, tiled=True),
        lax.all_gather(d_skip, "grp", axis=0, tiled=True),
        lax.all_gather(norm_gain, "grp", axis=0, tiled=True),
        lax.all_gather(w_out, "grp", axis=0, tiled=True),
    )
    gain_pre = gathered[0].astype(jnp.float32)
    conv_weight = gathered[3].astype(jnp.float32)
    conv_bias = gathered[4].astype(jnp.float32)
    bias_dt = gathered[5].astype(jnp.float32)
    log_rate = gathered[6].astype(jnp.float32)
    skip_gain = gathered[7].astype(jnp.float32)
    gain_norm = gathered[8].astype(jnp.float32)
    flat_in = inputs.reshape(tok_rows, model_width).astype(jnp.float32)
    normed_in, prenorm_back = jax.vjp(rms_scale, flat_in, gain_pre)
    hidden_low = normed_in.astype(jnp.bfloat16)
    projected = jnp.dot(hidden_low, gathered[1], preferred_element_type=jnp.float32)
    dt_linear = jnp.dot(hidden_low, gathered[2], preferred_element_type=jnp.float32)
    gate_rows = projected[:, :E]
    xbc_piece = projected[:, E:].reshape(seq_count, piece_len, E + 2 * N)
    rim_rows = passed_along(xbc_piece[:, piece_len - rim_len :, :], "grp", 1)
    mixed_parts, mix_back = jax.vjp(
        mix_inputs,
        xbc_piece,
        rim_rows,
        dt_linear.reshape(seq_count, piece_len, H),
        conv_weight,
        conv_bias,
        bias_dt,
        log_rate,
    )
    heads_x, b_rows, c_rows, step_size, decay_rate = mixed_parts
    (states, decays), stats_back = jax.vjp(block_stats, heads_x, b_rows, step_size, decay_rate)
    states = states.reshape(seq_count, per_seq, H, P_SIZE, N)
    decays = decays.reshape(seq_count, per_seq, H)
    local_starts, local_final = chain_forward(states, decays)
    prefix = jnp.cumprod(decays, axis=1)
    entering = prefix_2(
        (prefix[:, -1], local_final),
        "grp",
        join_states,
        (jnp.ones_like(prefix[:, -1]), jnp.zeros_like(local_final)),
        False,
    )[1]
    before = jnp.concatenate([jnp.ones_like(prefix[:, :1]), prefix[:, :-1]], axis=1)
    starts = local_starts + before[..., None, None] * entering[:, None]
    normed_out, mixer_back = jax.vjp(
        mixer_out,
        heads_x,
        b_rows,
        c_rows,
        step_size,
        decay_rate,
        starts.reshape(-1, H, P_SIZE, N),
        skip_gain,
        gate_rows,
        gain_norm,
    )
    out_low = normed_out.astype(jnp.bfloat16)
    result = (
        (flat_in + jnp.dot(out_low, gathered[9], preferred_element_type=jnp.float32))
        .astype(jnp.bfloat16)
        .reshape(seq_count, piece_len, model_width)
    )
    back_weights = (
        lax.all_gather(pre_gain, "grp", axis=0, tiled=True),
        lax.all_gather(w_in, "grp", axis=0, tiled=True),
        lax.all_gather(w_dt, "grp", axis=0, tiled=True),
        lax.all_gather(conv_w, "grp", axis=1, tiled=True),
        lax.all_gather(conv_b, "grp", axis=0, tiled=True),
        lax.all_gather(dt_bias, "grp", axis=0, tiled=True),
        lax.all_gather(a_log, "grp", axis=0, tiled=True),
        lax.all_gather(d_skip, "grp", axis=0, tiled=True),
        lax.all_gather(norm_gain, "grp", axis=0, tiled=True),
        lax.all_gather(w_out, "grp", axis=0, tiled=True),
    )
    cot_low = cotangent.reshape(tok_rows, model_width)
    d_normed = jnp.dot(cot_low, back_weights[9].T, preferred_element_type=jnp.float32)
    grad_out_w = jnp.dot(out_low.T, cot_low, preferred_element_type=jnp.float32)
    g_heads, g_brows, g_crows, g_step, g_rate, g_starts, g_skip, g_gate, g_norm = mixer_back(
        d_normed
    )
    after_local, first_local = chain_back(
        g_starts.reshape(seq_count, per_seq, H, P_SIZE, N), decays
    )
    suffix = jnp.flip(jnp.cumprod(jnp.flip(decays, 1), 1), 1)
    leaving = prefix_2(
        (suffix[:, 0], first_local),
        "grp",
        join_states,
        (jnp.ones_like(suffix[:, 0]), jnp.zeros_like(first_local)),
        True,
    )[1]
    suffix_after = jnp.concatenate([suffix[:, 1:], jnp.ones_like(suffix[:, :1])], axis=1)
    grad_states = after_local + suffix_after[..., None, None] * leaving[:, None]
    grad_decays = jnp.sum(grad_states * starts, axis=(-2, -1))
    g_xstat, g_bstat, g_sstat, g_rstat = stats_back(
        (grad_states.reshape(-1, H, P_SIZE, N), grad_decays.reshape(-1, H))
    )
    d_xbc, d_rim, d_dtlin, grad_conv_w, grad_conv_b, grad_bias_dt, grad_log_rate = mix_back(
        (g_heads + g_xstat, g_brows + g_bstat, g_crows, g_step + g_sstat, g_rate + g_rstat)
    )
    returned_rim = passed_along(d_rim, "grp", -1)
    d_xbc = jnp.concatenate(
        [d_xbc[:, : piece_len - rim_len], d_xbc[:, piece_len - rim_len :] + returned_rim], axis=1
    )
    d_proj = jnp.concatenate([g_gate, d_xbc.reshape(tok_rows, E + 2 * N)], axis=1).astype(
        jnp.bfloat16
    )
    d_step_low = d_dtlin.reshape(tok_rows, H).astype(jnp.bfloat16)
    grad_in_w = jnp.dot(hidden_low.T, d_proj, preferred_element_type=jnp.float32)
    grad_dt_w = jnp.dot(hidden_low.T, d_step_low, preferred_element_type=jnp.float32)
    d_hidden = jnp.dot(d_proj, back_weights[1].T, preferred_element_type=jnp.float32) + jnp.dot(
        d_step_low, back_weights[2].T, preferred_element_type=jnp.float32
    )
    d_flat, grad_pre = prenorm_back(d_hidden)
    d_inputs = (
        (cot_low.astype(jnp.float32) + d_flat)
        .astype(jnp.bfloat16)
        .reshape(seq_count, piece_len, model_width)
    )
    group_sums = (
        lax.psum_scatter(grad_pre, "grp", scatter_dimension=0, tiled=True),
        lax.psum_scatter(grad_in_w, "grp", scatter_dimension=0, tiled=True),
        lax.psum_scatter(grad_dt_w, "grp", scatter_dimension=0, tiled=True),
        lax.psum_scatter(grad_conv_w, "grp", scatter_dimension=1, tiled=True),
        lax.psum_scatter(grad_conv_b, "grp", scatter_dimension=0, tiled=True),
        lax.psum_scatter(grad_bias_dt, "grp", scatter_dimension=0, tiled=True),
        lax.psum_scatter(grad_log_rate, "grp", scatter_dimension=0, tiled=True),
        lax.psum_scatter(g_skip, "grp", scatter_dimension=0, tiled=True),
        lax.psum_scatter(g_norm, "grp", scatter_dimension=0, tiled=True),
        lax.psum_scatter(grad_out_w, "grp", scatter_dimension=0, tiled=True),
    )
    shares = lax.psum(
        (
            group_sums[0],
            group_sums[1],
            group_sums[2],
            group_sums[3],
            group_sums[4],
            group_sums[5],
            group_sums[6],
            group_sums[7],
            group_sums[8],
            group_sums[9],
        ),
        "rep",
    )
    return (
        result,
        d_inputs,
        shares[0],
        shares[1],
        shares[2],
        shares[3],
        shares[4],
        shares[5],
        shares[6],
        shares[7],
        shares[8],
        shares[9],
    )


def solution(mesh):
    in_specs = (
        P("rep", "grp", None),
        P("grp"),
        P("grp", None),
        P("grp", None),
        P(None, "grp"),
        P("grp"),
        P("grp"),
        P("grp"),
        P("grp"),
        P("grp"),
        P("grp", None),
        P("rep", "grp", None),
    )
    out_specs = (
        P("rep", "grp", None),
        P("rep", "grp", None),
        P("grp"),
        P("grp", None),
        P("grp", None),
        P(None, "grp"),
        P("grp"),
        P("grp"),
        P("grp"),
        P("grp"),
        P("grp"),
        P("grp", None),
    )
    return jax.shard_map(
        per_device, mesh=mesh, in_specs=in_specs, out_specs=out_specs, check_vma=False
    )
```

profile of v0, /device:TPU:0, one launch (start us, length us, event | category | flops | bytes accessed | tf_op | source)
XLA Modules:
  0.0 1036.1 jit_solution(11378324056444430992)
XLA Ops:
  47.5 32.5 %all-gather.12.cloned.1.call-done = bf16[768,3328]{1,0:T(8,128)(2,1)} async-done(((bf16[384,3328]{1,0:T(8,128)(2,1)}), bf16[768,3328]{1,0:T(8,128)(2,1)}) %all-gather.12.cloned.1.call-update) | async-done | bytes 5111824 | tf_op jit(solution)/shard_map/all_gather | solution.py:149
  97.4 14.9 %fusion.76 = (f32[2,512,1792]{2,1,0:T(8,128)S(1)}, f32[2,512,1792]{2,1,0:T(8,128)}) fusion(f32[2,512,1792]{2,1,0:T(8,128)} %bitcast.457, f32[1792]{0:T(1024)S(1)} %get-tuple-element.835, f32[2,3,1792]{2,1,0:T(4,128)S(1)} %copy.285, f32[1792]{0:T(1024)S(1)} %get-tuple-element.836, f32[1792]{0:T(1024)S(1)} %get-tuple-element.837, ...), kind=kLoop, calls=%fused_computation.121 | loop fusion | flops 27525120 | bytes 22098944 | tf_op jit(solution)/shard_map/jvp(jit(silu))/mul | solution.py:52
  116.7 10.2 reshape.530
  166.7 36.1 %all-gather.16.cloned.1.call-done = f32[4,24,64,128]{3,2,1,0:T(8,128)} async-done(((f32[2,24,64,128]{3,2,1,0:T(8,128)}), f32[4,24,64,128]{3,2,1,0:T(8,128)}) %all-gather.16.cloned.1.call-update) | async-done | bytes 3145744 | tf_op jit(solution)/shard_map/all_gather | solution.py:25
  210.6 61.2 %while.78 = (s32[]{:T(128)}, f32[4,256,24,64]{1,3,2,0:T(8,128)}, f32[4,256,24,64]{1,3,2,0:T(8,128)}, f32[4,256,128]{2,1,0:T(8,128)}, f32[4,256,128]{2,1,0:T(8,12...) while((s32[]{:T(128)}, f32[4,256,24,64]{1,3,2,0:T(8,128)}, ...), condition=%wide.region_9.10_spmd.clone.clone, body=%wide.region_6.9_spmd.clone.clone.sunk | while | flops 1922177152 | bytes 8869073 | solution.py:88
  271.8 10.6 %multiply_add_fusion.2 = f32[4,256,24,64]{1,3,2,0:T(8,128)} fusion(f32[4,256,24,64]{1,3,2,0:T(8,128)} %get-tuple-element.542, f32[4,256,24,64]{1,3,2,0:T(8,128)} %get-tuple-element.1348, f32[24]{0:T(128)S(1)} %convert_element_type.101), kind=kLoop, calls=%fused_computation.137 | loop fusion | flops 3145728 | bytes 18874464 | tf_op jit(solution)/shard_map/jvp()/add | solution.py:91
  292.2 11.1 %reshape.531 = f32[1024,1536]{1,0:T(8,128)} reshape(f32[4,256,24,64]{3,2,1,0:T(8,128)} %copy.338) | data formatting | bytes 12582912 | tf_op jit(solution)/shard_map/jvp()/reshape | solution.py:92
  311.0 10.2 multiply_reduce_fusion.7
  321.3 11.6 %fusion.80 = (f32[1536]{0:T(1024)}, f32[1024,1536]{1,0:T(8,128)}, bf16[1024,1536]{1,0:T(8,128)(2,1)}) fusion(f32[2,512,1536]{2,1,0:T(8,128)} %slice.169, f32[1024,3328]{1,0:T(8,128)} %copy-done.6, f32[1024,1536]{1,0:T(8,128)S(1)} %copy-done.12, f32[1024]{0:T(1024)S(1)} %multiply_multiply_fusion.3, f32[1024]{0:T(1024)S(1)} %fusion.136, ...), kind=kLoop, calls=%fused_computation.128 | loop fusion | flops 31455744 | bytes 40914944 | tf_op jit(solution)/shard_map/transpose(jvp())/reduce_sum | solution.py:91
  332.9 10.0 reshape.532
  361.1 187.7 %while.77 = (s32[]{:T(128)}, f32[4,256,24,64]{1,3,2,0:T(8,128)}, f32[4,256,128]{2,1,0:T(8,128)}, f32[4,256,128]{2,1,0:T(8,128)}, f32[4,256,24]{1,2,0:T(8,128)}, ...) while((s32[]{:T(128)}, f32[4,256,24,64]{1,3,2,0:T(8,128)}, ...), condition=%wide.region_22.23_spmd, body=%wide.region_12.22_spmd.sunk | while | flops 4564555776 | bytes 31272272 | solution.py:88
  372.5 12.8 %fusion.232 = (f32[24,256]{1,0:T(8,128)S(1)}, f32[24,256]{1,0:T(8,128)S(1)}, f32[24,256]{1,0:T(8,128)}, f32[256,256]{1,0:T(8,128)}) fusion(f32[24,256]{1,0:T(8,128)} %bitcast.480, f32[256,256]{1,0:T(8,128)S(1)} %fusion.230, f32[24,256]{1,0:T(8,128)S(1)} %copy_bitcast_fusion.13, f32[256,256]{1,0:T(8,128)} %fusion.231, ...), kind=kOutput, calls=%fused_computation.16.clone.1 | convolution fusion | flops 1231468544 | bytes 4055040 | tf_op jit(solution)/shard_map/transpose(jvp())/while/body/eval_jaxpr/checkpoint/hts,shp->thp/dot_general | solution.py:80
  419.3 12.8 %fusion.232 = (f32[24,256]{1,0:T(8,128)S(1)}, f32[24,256]{1,0:T(8,128)S(1)}, f32[24,256]{1,0:T(8,128)}, f32[256,256]{1,0:T(8,128)}) fusion(f32[24,256]{1,0:T(8,128)} %bitcast.480, f32[256,256]{1,0:T(8,128)S(1)} %fusion.230, f32[24,256]{1,0:T(8,128)S(1)} %copy_bitcast_fusion.13, f32[256,256]{1,0:T(8,128)} %fusion.231, ...), kind=kOutput, calls=%fused_computation.16.clone.1 | convolution fusion | flops 1231468544 | bytes 4055040 | tf_op jit(solution)/shard_map/transpose(jvp())/while/body/eval_jaxpr/checkpoint/hts,shp->thp/dot_general | solution.py:80
  466.0 12.8 %fusion.232 = (f32[24,256]{1,0:T(8,128)S(1)}, f32[24,256]{1,0:T(8,128)S(1)}, f32[24,256]{1,0:T(8,128)}, f32[256,256]{1,0:T(8,128)}) fusion(f32[24,256]{1,0:T(8,128)} %bitcast.480, f32[256,256]{1,0:T(8,128)S(1)} %fusion.230, f32[24,256]{1,0:T(8,128)S(1)} %copy_bitcast_fusion.13, f32[256,256]{1,0:T(8,128)} %fusion.231, ...), kind=kOutput, calls=%fused_computation.16.clone.1 | convolution fusion | flops 1231468544 | bytes 4055040 | tf_op jit(solution)/shard_map/transpose(jvp())/while/body/eval_jaxpr/checkpoint/hts,shp->thp/dot_general | solution.py:80
  512.8 12.8 %fusion.232 = (f32[24,256]{1,0:T(8,128)S(1)}, f32[24,256]{1,0:T(8,128)S(1)}, f32[24,256]{1,0:T(8,128)}, f32[256,256]{1,0:T(8,128)}) fusion(f32[24,256]{1,0:T(8,128)} %bitcast.480, f32[256,256]{1,0:T(8,128)S(1)} %fusion.230, f32[24,256]{1,0:T(8,128)S(1)} %copy_bitcast_fusion.13, f32[256,256]{1,0:T(8,128)} %fusion.231, ...), kind=kOutput, calls=%fused_computation.16.clone.1 | convolution fusion | flops 1231468544 | bytes 4055040 | tf_op jit(solution)/shard_map/transpose(jvp())/while/body/eval_jaxpr/checkpoint/hts,shp->thp/dot_general | solution.py:80
  572.3 32.2 %all-gather.18.cloned.1.call-done = f32[4,24,64,128]{3,2,1,0:T(8,128)} async-done(((f32[2,24,64,128]{3,2,1,0:T(8,128)}), f32[4,24,64,128]{3,2,1,0:T(8,128)}) %all-gather.18.cloned.1.call-update) | async-done | bytes 3145744 | tf_op jit(solution)/shard_map/all_gather | solution.py:25
  611.7 11.0 %multiply_reduce_fusion.8 = (f32[4,256,24]{1,2,0:T(8,128)S(1)}, f32[4,256,24,64]{1,3,2,0:T(8,128)}) fusion(f32[4,256,24,64]{1,3,2,0:T(8,128)S(1)} %bitcast.453, f32[4,256,24]{1,2,0:T(8,128)S(1)} %copy-done.29, f32[4,256,24,64]{1,3,2,0:T(8,128)} %get-tuple-element.548, f32[4,256,24,64]{1,3,2,0:T(8,128)S(1)} %bitcast.455, f32[24]{0:T(128)S(1)} %copy-done.81, ...), kind=kOutput, calls=%fused_computation.130 | convolution fusion | flops 2425331712 | bytes 29032544 | tf_op jit(solution)/shard_map/transpose(jvp(mqhp,mqn->mhpn))/dot_general | solution.py:65
  622.7 10.0 copy.331
  632.7 11.6 %reshape.521 = f32[2,512,1536]{2,1,0:T(8,128)} reshape(f32[4,256,24,64]{3,2,1,0:T(8,128)} %copy.331) | data formatting | bytes 12582912 | tf_op jit(solution)/shard_map/transpose(jvp())/reshape | solution.py:54
  644.3 12.4 %fusion.107 = f32[4,256,128]{2,1,0:T(8,128)S(1)} fusion(f32[4,256,128]{2,1,0:T(8,128)} %get-tuple-element.544, f32[4,24,64,128]{3,2,1,0:T(8,128)S(1)} %bitcast.464, f32[4,256,24,64]{1,3,2,0:T(8,128)} %get-tuple-element.1349, f32[4,256,24]{1,2,0:T(8,128)S(1)} %copy-done.29), kind=kOutput, calls=%fused_computation.180 | convolution fusion | flops 2417623040 | bytes 10584064 | tf_op jit(solution)/shard_map/transpose(jvp(mqhp,mqn->mhpn))/dot_general | solution.py:65
  656.8 16.6 %multiply_reduce_fusion.5 = (f32[1792]{0:T(1024)S(1)}, f32[1792]{0:T(1024)S(1)}, f32[1792]{0:T(1024)S(1)}, f32[1792]{0:T(1024)S(1)}, f32[1792]{0:T(1024)S(1)}, /*index=5*/f32[2,512,1792]{2,1,0:T(8,128)}) fusion(f32[2,512,1792]{2,1,0:T(8,128)} %bitcast.458, f32[2,3,1792]{2,1,0:T(4,128)S(1)} %copy-done.36, f32[1024,3328]{1,0:T(8,128)} %copy-done.6, ...), kind=kLoop, calls=%fused_computation.118 | loop fusion | flops 42196224 | bytes 36779008 | tf_op jit(solution)/shard_map/transpose(jvp())/reduce_sum | solution.py:51
  725.2 102.7 %reduce-scatter.7.cloned.1.call-done = f32[384,3328]{1,0:T(8,128)} async-done(((f32[768,3328]{1,0:T(8,128)}), f32[384,3328]{1,0:T(8,128)}) %reduce-scatter.7.cloned.1.call-update) | async-done | bytes 5111824 | tf_op jit(solution)/shard_map/reduce_scatter | solution.py:276
  862.0 64.8 %all-reduce.23 = (f32[384]{0:T(512)}, f32[384,24]{0,1:T(8,128)}, f32[4,896]{1,0:T(4,128)}, f32[896]{0:T(1024)}, f32[12]{0:T(128)}, /*index=5*/f32[12]{0:T(128)}, f32[12]{0:T(128)}, f32[768]{0:T(1024)}) all-reduce(f32[384]{0:T(512)S(1)} %dynamic-slice.4, ...), channel_id=1, replica_groups=mesh['rep'=16,'grp'=2] {'rep'}, use_global_device_ids=true, to_apply=%region_34.35 | all-reduce | flops 14884 | bytes 119072 | tf_op jit(solution)/shard_map/psum | solution.py:286
  926.7 96.0 %all-reduce.29.cloned.1.call-done = (f32[384,3328]{1,0:T(8,128)}, f32[768,768]{1,0:T(8,128)}) async-done(((f32[384,3328]{1,0:T(8,128)}, f32[768,768]{1,0:T(8,128)}), (f32[384,3328]{1,0:T(8,128)}, f32[768,768]{1,0:T(8,128)})) %all-reduce.29.cloned.1.call-update) | async-done | bytes 7471120 | tf_op jit(solution)/shard_map/psum | solution.py:286
  (540 shorter events, 473.7 us)
Async XLA Ops:
  7.2 72.8 %all-gather.12.cloned.1.call-start = ((), (), s32[]{:S(2)}) async-start(), calls=%async_computation.4 | async-start | bytes 7667712 | tf_op jit(solution)/shard_map/all_gather | solution.py:149
  7.9 194.9 %all-gather.16.cloned.1.call-start = ((), (), s32[]{:S(2)}) async-start(), calls=%async_computation.9 | async-start | bytes 4718592 | tf_op jit(solution)/shard_map/all_gather | solution.py:25
  23.4 65.0 %copy-start.55 = (f32[768]{0:T(1024)}, f32[768]{0:T(1024)S(1)}, u32[]{:S(2)}) copy-start(f32[768]{0:T(1024)S(1)} %reshape.504) | copy-start | bytes 9220
  33.2 123.3 %copy-start.20 = (f32[4,256,24]{1,0,2:T(4,128)}, f32[4,256,24]{1,0,2:T(4,128)S(1)}, u32[]{:S(2)}) copy-start(f32[4,256,24]{1,0,2:T(4,128)S(1)} %reshape.447) | copy-start | bytes 294916
  33.2 123.3 %copy-start.74 = (f32[24]{0:T(128)}, f32[24]{0:T(128)S(1)}, u32[]{:S(2)}) copy-start(f32[24]{0:T(128)S(1)} %convert_exponential_fusion) | copy-start | bytes 292
  35.6 52.8 %copy-start.22 = (f32[4,24,2,128]{3,1,2,0:T(8,128)}, f32[4,24,2,128]{3,1,2,0:T(8,128)S(1)}, u32[]{:S(2)}) copy-start(f32[4,24,2,128]{3,1,2,0:T(8,128)S(1)} %reduce-window.74) | copy-start | bytes 294916
  35.8 52.6 %copy-start.44 = (f32[4,24,2]{1,2,0:T(2,128)}, f32[4,24,2]{1,2,0:T(2,128)S(1)}, u32[]{:S(2)}) copy-start(f32[4,24,2]{1,2,0:T(2,128)S(1)} %copy.291) | copy-start | bytes 2308
  36.4 52.0 %copy-start.57 = (f32[1024]{0:T(1024)}, f32[1024]{0:T(1024)S(1)}, u32[]{:S(2)}) copy-start(f32[1024]{0:T(1024)S(1)} %rsqrt.23) | copy-start | bytes 12292
  45.6 111.6 %copy-start.63 = (f32[4,24]{1,0:T(4,128)}, f32[4,24]{1,0:T(4,128)S(1)}, u32[]{:S(2)}) copy-start(f32[4,24]{1,0:T(4,128)S(1)} %get-tuple-element.833) | copy-start | bytes 1156
  45.7 51.6 %copy-start.47 = (f32[1792]{0:T(1024)}, f32[1792]{0:T(1024)S(1)}, u32[]{:S(2)}) copy-start(f32[1792]{0:T(1024)S(1)} %get-tuple-element.834) | copy-start | bytes 21508
  45.7 51.6 %copy-start.49 = (f32[1792]{0:T(1024)}, f32[1792]{0:T(1024)S(1)}, u32[]{:S(2)}) copy-start(f32[1792]{0:T(1024)S(1)} %get-tuple-element.835) | copy-start | bytes 21508
  45.9 90.7 %copy-start.28 = (f32[4,256,24]{1,2,0:T(8,128)}, f32[4,256,24]{1,2,0:T(8,128)S(1)}, u32[]{:S(2)}) copy-start(f32[4,256,24]{1,2,0:T(8,128)S(1)} %get-tuple-element.953) | copy-start | bytes 294916
  93.4 3.9 collective-permute-start
  155.7 155.3 %all-gather.14.cloned.1.call-start = ((), (), s32[]{:S(2)}) async-start(), calls=%async_computation.5 | async-start | bytes 3538944 | tf_op jit(solution)/shard_map/all_gather | solution.py:157
  156.5 448.1 %all-gather.18.cloned.1.call-start = ((), (), s32[]{:S(2)}) async-start(), calls=%async_computation.10 | async-start | bytes 4718592 | tf_op jit(solution)/shard_map/all_gather | solution.py:25
  161.8 110.0 %copy-start.80 = (f32[24]{0:T(128)}, f32[24]{0:T(128)S(1)}, u32[]{:S(2)}) copy-start(f32[24]{0:T(128)S(1)} %convert_element_type.101) | copy-start | bytes 292
  166.7 154.5 %copy-start.65 = (f32[1536]{0:T(1024)}, f32[1536]{0:T(1024)S(1)}, u32[]{:S(2)}) copy-start(f32[1536]{0:T(1024)S(1)} %reshape.505) | copy-start | bytes 18436
  361.1 189.8 %copy-start = (f32[2,24,64,128]{3,2,1,0:T(8,128)S(1)}, f32[2,24,64,128]{3,2,1,0:T(8,128)}, u32[]{:S(2)}) copy-start(f32[2,24,64,128]{3,2,1,0:T(8,128)} %custom-call.1) | copy-start | bytes 4718596
  559.5 165.8 %reduce-scatter.11.cloned.1.call-start = ((), (), s32[]{:S(2)}) async-start(), calls=%async_computation.8 | async-start | bytes 7077888 | tf_op jit(solution)/shard_map/reduce_scatter | solution.py:284
  572.3 255.7 %reduce-scatter.7.cloned.1.call-start = ((), (), s32[]{:S(2)}) async-start(), calls=%async_computation.6 | async-start | bytes 15335424 | tf_op jit(solution)/shard_map/reduce_scatter | solution.py:276
  683.1 8.9 collective-permute-start.1
  707.1 150.8 %reduce-scatter.13.cloned.1.call-start = ((), (), s32[]{:S(2)}) async-start(), calls=%async_computation.11 | async-start | bytes 1376256
  720.7 141.3 %reduce-scatter.9.cloned.1.call-start = ((), (), s32[]{:S(2)}) async-start(), calls=%async_computation.7 | async-start | bytes 110592 | tf_op jit(solution)/shard_map/reduce_scatter | solution.py:277
  722.2 300.5 %all-reduce.29.cloned.1.call-start = ((), (), s32[]{:S(2)}) async-start(), calls=%async_computation.12 | async-start | bytes 14942208 | tf_op jit(solution)/shard_map/psum | solution.py:286
  (90 other events, 1157.9 us)
Sparse Core Ops, SparseCore 0:
  9.6 70.3 all-gather.11
  155.8 46.9 all-gather.15
  204.4 36.0 all-gather.13
  559.6 44.9 all-gather.17
  607.3 59.9 reduce-scatter.10
  707.2 120.6 reduce-scatter.6
  830.9 18.8 reduce-scatter.12
  852.0 9.9 reduce-scatter.8
  865.7 156.9 all-reduce.28
where the time goes:
time: 1050 us; the launch traced here: 1040 us
  waiting for transfers between devices  305 us (29%)
  matrix products  276 us (26%)
  local copies, waits for them, and re-layouts  179 us (17%)
  other arithmetic  142 us (14%)
  blocking collectives  109 us (10%)
  between operations  18.7 us (2%)
    dot_general x12, matrix products, block_out(): jnp.einsum('hts,shp->thp', mixing, heads_x, precision=exact_mode)  117 us
    reduce_scatter x1, waiting for transfers between devices, per_device(): lax.psum_scatter(grad_in_w, 'grp', scatter_dimension=0, tiled=True)  103 us
    psum x1, waiting for transfers between devices, per_device(): lax.psum((group_sums[0], group_sums[1], group_sums[2], group_sums[3], gro...  96 us
    all_gather x2, waiting for transfers between devices, prefix_2(): pieces = jax.tree.map(lambda part: lax.all_gather(part, axis), value)  68.4 us
    psum x1, blocking collectives, per_device(): lax.psum((group_sums[0], group_sums[1], group_sums[2], group_sums[3], gro...  64.8 us
    dot_general x16, matrix products, block_out(): jnp.einsum('tn,hpn->thp', c_rows, start_state, precision=exact_mode)  43.7 us
    unnamed x198, local copies, waits for them, and re-layouts  39 us
    all_gather x1, waiting for transfers between devices, per_device(): lax.all_gather(w_in, 'grp', axis=0, tiled=True)  32.5 us
  transfers between devices with their start and end apart: 11, of which 7 were waited for; matrix products, arithmetic and copies ran while one was open for 25% of the time, Pallas kernels for 0%

commit v1 on v0

v1 whole, which is shorter than its diff:
```python
import jax
import jax.numpy as jnp
from jax import lax
from jax.experimental import pallas as pl
from jax.experimental.pallas import tpu as pltpu
from jax.sharding import PartitionSpec as P

E = 1536
H = 24
P_SIZE = 64
N = 128
K = 4
BLOCK = 256
CH = E + 2 * N
PAD = 128
EPS = 1e-05
FAR = -1e30
SEND = jnp.bfloat16
VMEM = 56 * 1024 * 1024

f32 = jnp.float32
bf16 = jnp.bfloat16


def nn(a, b):
    return lax.dot_general(a, b, (((1,), (0,)), ((), ())), preferred_element_type=f32)


def nt(a, b):
    return lax.dot_general(a, b, (((1,), (1,)), ((), ())), preferred_element_type=f32)


def tn(a, b):
    return lax.dot_general(a, b, (((0,), (0,)), ((), ())), preferred_element_type=f32)


def split2(v):
    hi = v.astype(bf16)
    return hi, (v - hi.astype(f32)).astype(bf16)


def split3(v):
    hi = v.astype(bf16)
    rest = v - hi.astype(f32)
    mid = rest.astype(bf16)
    return hi, mid, (rest - mid.astype(f32)).astype(bf16)


def triangle(lower):
    row = lax.broadcasted_iota(jnp.int32, (BLOCK, BLOCK), 0)
    col = lax.broadcasted_iota(jnp.int32, (BLOCK, BLOCK), 1)
    return row >= col if lower else col >= row


def running_sum(mask, v):
    ones = jnp.where(mask, 1.0, 0.0).astype(bf16)
    hi, mid, lo = split3(v)
    return nn(ones, hi) + nn(ones, mid) + nn(ones, lo)


def spread_heads(v, heads2):
    return nn(jnp.concatenate(split2(v), axis=1), heads2)


def sum_heads(v, heads):
    hi, lo = split2(v)
    return nt(hi, heads) + nt(lo, heads)


def softplus(v):
    return jnp.maximum(v, 0.0) + jnp.log1p(jnp.exp(-jnp.abs(v)))


def sigmoid(v):
    return 1.0 / (1.0 + jnp.exp(-v))


def rates(dt, bias, log_rate):
    step = softplus(dt + bias)
    rate = -step * jnp.exp(log_rate)
    cum = running_sum(triangle(True), rate)
    return step, rate, cum


def conv_sum(ext, conv_w, conv_b):
    summed = conv_b
    for k in range(K):
        summed = summed + conv_w[k : k + 1, :] * ext[5 + k : 5 + k + BLOCK, :]
    return summed


def forward_kernel(
    in_ref, cot_ref, pre_ref, w_in_ref, w_dt_ref, cw_ref, cb_ref, bias_ref, log_ref, skip_ref,
    gain_ref, w_out_ref, heads2_ref,
    hid_o, xbc_o, dt_o, norm_o, dgate_o, dy_o, r1_o, start_o, gain_o, skip_o,
    ext, state, inner,
):
    first = pl.program_id(0) == 0

    @pl.when(first)
    def _():
        ext[0:8, :] = jnp.zeros((8, CH), f32)
        state[...] = jnp.zeros_like(state)
        gain_o[...] = jnp.zeros_like(gain_o)
        skip_o[...] = jnp.zeros_like(skip_o)

    values = in_ref[...].astype(f32)
    scale = lax.rsqrt(jnp.mean(values * values, axis=-1, keepdims=True) + EPS)
    hidden = (values * scale * pre_ref[...]).astype(bf16)
    hid_o[...] = hidden
    xbc = nn(hidden, w_in_ref[:, E:])
    xbc_o[...] = xbc
    ext[8:, :] = xbc
    dt = nn(hidden, w_dt_ref[...])
    dt_o[...] = dt
    step, rate, cum = rates(dt, bias_ref[...], log_ref[...])
    last = cum[BLOCK - 1 : BLOCK, :]
    cum_t = cum.T
    summed = conv_sum(ext, cw_ref[...], cb_ref[...])
    tail = ext[BLOCK : BLOCK + 8, :]
    ext[0:8, :] = tail
    mixed = summed * sigmoid(summed)
    x = mixed[:, :E]
    b = mixed[:, E : E + N].astype(bf16)
    c = mixed[:, E + N :].astype(bf16)
    heads2 = heads2_ref[...]
    xd = (x * spread_heads(step, heads2)).astype(bf16)
    scores = nt(c, b)
    mask = triangle(True)
    low_lane = lax.broadcasted_iota(jnp.int32, (BLOCK, PAD), 1) < P_SIZE
    for pair in range(H // 2):
        lanes = slice(pair * PAD, (pair + 1) * PAD)
        part = xd[:, lanes]
        total = None
        for side in range(2):
            h = 2 * pair + side
            far = jnp.where(mask, cum[:, h : h + 1] - cum_t[h : h + 1, :], FAR)
            mixing = (scores * jnp.exp(far)).astype(bf16)
            keep = low_lane if side == 0 else jnp.logical_not(low_lane)
            one = nn(mixing, jnp.where(keep, part, jnp.zeros_like(part)))
            total = one if total is None else total + one
        inner[:, lanes] = total
    start = state[...].astype(bf16)
    start_o[0] = start
    y_inner = inner[...] + nn(c, start) * spread_heads(jnp.exp(cum), heads2)
    to_last = (xd.astype(f32) * spread_heads(jnp.exp(last - cum), heads2)).astype(bf16)
    whole = spread_heads(jnp.broadcast_to(jnp.exp(last), (8, PAD)), heads2)[0:1, :]
    state[...] = whole * state[...] + tn(b, to_last)

    y = y_inner + skip_ref[...] * x
    gate = nn(hidden, w_in_ref[:, :E])
    sig = sigmoid(gate)
    opened = gate * sig
    gated = y * opened
    out_scale = lax.rsqrt(jnp.mean(gated * gated, axis=-1, keepdims=True) + EPS)
    unit = gated * out_scale
    gain = gain_ref[...]
    norm_o[...] = (unit * gain).astype(bf16)
    d_normed = nt(cot_ref[...], w_out_ref[...])
    gain_o[...] += jnp.sum(d_normed * unit, axis=0, keepdims=True)
    d_unit = d_normed * gain
    d_gated = out_scale * (d_unit - unit * jnp.mean(d_unit * unit, axis=-1, keepdims=True))
    dy = d_gated * opened
    dgate_o[...] = (d_gated * y * (sig + opened * (1.0 - sig))).astype(bf16)
    dy_low = dy.astype(bf16)
    dy_o[...] = dy_low
    r1_o[...] = sum_heads(dy_low.astype(f32) * y_inner, heads2[:PAD, :])
    skip_o[...] += jnp.sum(dy * x, axis=0, keepdims=True)


def backward_kernel(
    xbc_ref, before_ref, dt_ref, dy_ref, r1_ref, start_ref, cw_ref, cb_ref, bias_ref, log_ref,
    skip_ref, heads2_ref,
    dxbc_o, ddt_o, gcw_o, gcb_o, gbias_o, glog_o,
    ext, ext_back, d_state, d_inner, d_scores,
):
    step_id = pl.program_id(0)
    steps = pl.num_programs(0)

    @pl.when(step_id == 0)
    def _():
        ext_back[BLOCK:, :] = jnp.zeros((8, CH), f32)
        d_state[...] = jnp.zeros_like(d_state)
        gcw_o[...] = jnp.zeros_like(gcw_o)
        gcb_o[...] = jnp.zeros_like(gcb_o)
        gbias_o[...] = jnp.zeros_like(gbias_o)
        glog_o[...] = jnp.zeros_like(glog_o)

    xbc = xbc_ref[...]
    ext[0:8, :] = jnp.where(step_id == steps - 1, 0.0, before_ref[...])
    ext[8:, :] = xbc
    cw = cw_ref[...]
    summed = conv_sum(ext, cw, cb_ref[...])
    sig = sigmoid(summed)
    mixed = summed * sig
    d_silu = sig + mixed * (1.0 - sig)
    x = mixed[:, :E]
    b = mixed[:, E : E + N].astype(bf16)
    c = mixed[:, E + N :].astype(bf16)
    dt = dt_ref[...]
    step, rate, cum = rates(dt, bias_ref[...], log_ref[...])
    last = cum[BLOCK - 1 : BLOCK, :]
    cum_t = cum.T
    heads2 = heads2_ref[...]
    heads = heads2[:PAD, :]
    step_e = spread_heads(step, heads2)
    xd = (x * step_e).astype(bf16)
    dy = dy_ref[...]
    scores_t = nt(b, c)
    mask = triangle(False)
    low_lane = lax.broadcasted_iota(jnp.int32, (BLOCK, PAD), 1) < P_SIZE
    d_scores[...] = jnp.zeros_like(d_scores)
    for pair in range(H // 2):
        lanes = slice(pair * PAD, (pair + 1) * PAD)
        part = xd[:, lanes]
        dpart = dy[:, lanes]
        total = None
        for side in range(2):
            h = 2 * pair + side
            far = jnp.where(mask, cum_t[h : h + 1, :] - cum[:, h : h + 1], FAR)
            decay = jnp.exp(far)
            mixing = (scores_t * decay).astype(bf16)
            keep = low_lane if side == 0 else jnp.logical_not(low_lane)
            d_scores[...] += nt(jnp.where(keep, part, jnp.zeros_like(part)), dpart) * decay
            one = nn(mixing, jnp.where(keep, dpart, jnp.zeros_like(dpart)))
            total = one if total is None else total + one
        d_inner[:, lanes] = total
    start = start_ref[0]
    d_last = d_state[...]
    d_last_low = d_last.astype(bf16)
    to_last = spread_heads(jnp.exp(last - cum), heads2)
    carried = to_last * nn(b, d_last_low)
    dxd = d_inner[...] + carried
    xd32 = xd.astype(f32)
    whole = spread_heads(jnp.broadcast_to(jnp.exp(last), (8, PAD)), heads2)[0:1, :]
    end_row = jnp.sum(xd32 * carried, axis=0, keepdims=True) + whole * jnp.sum(
        d_last * start.astype(f32), axis=0, keepdims=True
    )
    r3 = sum_heads(jnp.broadcast_to(end_row, (8, E)), heads)[0:1, :]
    row = lax.broadcasted_iota(jnp.int32, (BLOCK, PAD), 0)
    d_cum = r1_ref[...] - sum_heads(xd32 * dxd, heads) + jnp.where(row == BLOCK - 1, r3, 0.0)
    d_rate = running_sum(triangle(False), d_cum)
    d_step = sum_heads(dxd * x, heads) - jnp.exp(log_ref[...]) * d_rate
    glog_o[...] += jnp.sum(d_rate * rate, axis=0, keepdims=True)
    ddt = d_step * sigmoid(dt + bias_ref[...])
    gbias_o[...] += jnp.sum(ddt, axis=0, keepdims=True)
    ddt_o[...] = ddt.astype(bf16)
    dy32 = dy.astype(f32)
    dx = dxd * step_e + skip_ref[...] * dy32
    dy_e = (dy32 * spread_heads(jnp.exp(cum), heads2)).astype(bf16)
    weighted = (xd32 * to_last).astype(bf16)
    d_sc = d_scores[...].astype(bf16)
    d_c = tn(d_sc, b) + nt(dy_e, start)
    d_b = nn(d_sc, c) + nt(weighted, d_last_low)
    d_state[...] = whole * d_last + tn(c, dy_e)
    d_sum = jnp.concatenate([dx, d_b, d_c], axis=1) * d_silu
    gcb_o[...] += jnp.sum(d_sum, axis=0, keepdims=True)
    ext_back[0:BLOCK, :] = d_sum
    total = None
    for k in range(K):
        later = ext_back[K - 1 - k : K - 1 - k + BLOCK, :]
        gcw_o[k : k + 1, :] += jnp.sum(xbc * later, axis=0, keepdims=True)
        one = cw[k : k + 1, :] * later
        total = one if total is None else total + one
    dxbc_o[...] = total.astype(bf16)
    head = ext_back[0:8, :]
    ext_back[BLOCK:, :] = head


def whole_spec(shape):
    return pl.BlockSpec(shape, lambda i: tuple(0 for _ in shape))


def forward_call(seq, cot, pre, w_in, w_dt, cw, cb, bias, log_rate, skip, gain, w_out, heads2):
    tokens, width = seq.shape
    blocks = tokens // BLOCK
    rows = lambda n: pl.BlockSpec((BLOCK, n), lambda i: (i, 0))
    out = jax.ShapeDtypeStruct
    weights = (pre, w_in, w_dt, cw, cb, bias, log_rate, skip, gain, w_out, heads2)
    return pl.pallas_call(
        forward_kernel,
        grid=(blocks,),
        in_specs=[rows(width), rows(width)] + [whole_spec(w.shape) for w in weights],
        out_specs=[
            rows(width), rows(CH), rows(PAD), rows(E), rows(E), rows(E), rows(PAD),
            pl.BlockSpec((1, N, E), lambda i: (i, 0, 0)),
            whole_spec((1, E)), whole_spec((1, E)),
        ],
        out_shape=[
            out((tokens, width), bf16), out((tokens, CH), f32), out((tokens, PAD), f32),
            out((tokens, E), bf16), out((tokens, E), bf16), out((tokens, E), bf16),
            out((tokens, PAD), f32), out((blocks, N, E), bf16), out((1, E), f32), out((1, E), f32),
        ],
        scratch_shapes=[
            pltpu.VMEM((BLOCK + 8, CH), f32), pltpu.VMEM((N, E), f32), pltpu.VMEM((BLOCK, E), f32),
        ],
        compiler_params=pltpu.CompilerParams(vmem_limit_bytes=VMEM),
        cost_estimate=pl.CostEstimate(
            flops=20_000_000_000, bytes_accessed=40_000_000, transcendentals=12_000_000
        ),
        name="mixer_forward",
    )(seq, cot, *weights)


def backward_call(xbc, dt, dy, r1, starts, cw, cb, bias, log_rate, skip, heads2):
    tokens = xbc.shape[0]
    blocks = tokens // BLOCK
    per = BLOCK // 8
    rows = lambda n: pl.BlockSpec((BLOCK, n), lambda i: (blocks - 1 - i, 0))
    out = jax.ShapeDtypeStruct
    weights = (cw, cb, bias, log_rate, skip, heads2)
    return pl.pallas_call(
        backward_kernel,
        grid=(blocks,),
        in_specs=[
            rows(CH),
            pl.BlockSpec((8, CH), lambda i: (jnp.maximum((blocks - 1 - i) * per - 1, 0), 0)),
            rows(PAD), rows(E), rows(PAD),
            pl.BlockSpec((1, N, E), lambda i: (blocks - 1 - i, 0, 0)),
        ]
        + [whole_spec(w.shape) for w in weights],
        out_specs=[
            rows(CH), rows(PAD), whole_spec((K, CH)), whole_spec((1, CH)), whole_spec((1, PAD)),
            whole_spec((1, PAD)),
        ],
        out_shape=[
            out((tokens, CH), bf16), out((tokens, PAD), bf16), out((K, CH), f32),
            out((1, CH), f32), out((1, PAD), f32), out((1, PAD), f32),
        ],
        scratch_shapes=[
            pltpu.VMEM((BLOCK + 8, CH), f32), pltpu.VMEM((BLOCK + 8, CH), f32),
            pltpu.VMEM((N, E), f32), pltpu.VMEM((BLOCK, E), f32), pltpu.VMEM((BLOCK, BLOCK), f32),
        ],
        compiler_params=pltpu.CompilerParams(vmem_limit_bytes=VMEM),
        cost_estimate=pl.CostEstimate(
            flops=20_000_000_000, bytes_accessed=30_000_000, transcendentals=12_000_000
        ),
        name="mixer_backward",
    )(xbc, xbc, dt, dy, r1, starts, *weights)


SWAP = [(0, 1), (1, 0)]


def to_sequence(pieces, mine):
    kept = lax.dynamic_index_in_dim(pieces, mine, 0, keepdims=False)
    other = lax.ppermute(lax.dynamic_index_in_dim(pieces, 1 - mine, 0, keepdims=False), "grp", SWAP)
    early = jnp.where(mine == 0, kept, other)
    late = jnp.where(mine == 0, other, kept)
    return jnp.concatenate([early, late], axis=0)


def to_pieces(seq, mine):
    halves = seq.reshape(2, seq.shape[0] // 2, seq.shape[1])
    kept = lax.dynamic_index_in_dim(halves, mine, 0, keepdims=False)
    other = lax.ppermute(lax.dynamic_index_in_dim(halves, 1 - mine, 0, keepdims=False), "grp", SWAP)
    return jnp.where(mine == 0, jnp.stack([kept, other]), jnp.stack([other, kept]))


def pad_heads(v):
    return jnp.pad(v, [(0, 0)] * (v.ndim - 1) + [(0, PAD - H)])


def reduced(grad):
    part = lax.psum_scatter(grad.astype(SEND), "grp", scatter_dimension=0, tiled=True)
    return lax.psum(part, "rep").astype(f32)


def per_device(
    inputs, pre_gain, w_in, w_dt, conv_w, conv_b, dt_bias, a_log, d_skip, norm_gain, w_out,
    cotangent,
):
    mine = lax.axis_index("grp")
    gather = lambda v, axis=0: lax.all_gather(v, "grp", axis=axis, tiled=True)
    vectors = jnp.concatenate(
        [conv_w.reshape(-1), pre_gain, conv_b, dt_bias, a_log, d_skip, norm_gain, w_dt.reshape(-1)]
    )
    both = lax.all_gather(vectors, "grp", axis=0)
    sizes = [conv_w.size, pre_gain.size, conv_b.size, H // 2, H // 2, H // 2, norm_gain.size]
    cuts, at = [], 0
    for size in sizes:
        cuts.append(both[:, at : at + size])
        at += size
    half = conv_w.shape[1]
    cw = cuts[0].reshape(2, K, half).transpose(1, 0, 2).reshape(K, CH).astype(f32)
    pre, cb, bias, log_rate, skip, gain = (v.reshape(1, -1).astype(f32) for v in cuts[1:])
    wdt = pad_heads(both[:, at:].reshape(-1, H))
    bias, log_rate = pad_heads(bias), pad_heads(log_rate)
    skip = jnp.repeat(skip, P_SIZE, axis=1)
    win = gather(w_in)
    wout = gather(w_out)
    heads = (jnp.arange(PAD)[:, None] == jnp.arange(E)[None, :] // P_SIZE).astype(bf16)
    heads2 = jnp.concatenate([heads, heads], axis=0)
    seq = to_sequence(inputs, mine)
    cot = to_sequence(cotangent, mine)
    hidden, xbc, dt, normed, d_gate, dy, r1, starts, g_gain, g_skip = forward_call(
        seq, cot, pre, win, wdt, cw, cb, bias, log_rate, skip, gain, wout, heads2
    )
    grad_out_w = reduced(tn(normed, cot))
    grad_gate_w = reduced(tn(hidden, d_gate))
    result = to_pieces((seq.astype(f32) + nn(normed, wout)).astype(bf16), mine)
    d_xbc, d_dt, g_cw, g_cb, g_bias, g_log = backward_call(
        xbc, dt, dy, r1, starts, cw, cb, bias, log_rate, skip, heads2
    )
    grad_xbc_w = reduced(tn(hidden, d_xbc))
    grad_in_w = jnp.concatenate([grad_gate_w, grad_xbc_w], axis=1)
    d_hidden = nt(d_gate, win[:, :E]) + nt(d_xbc, win[:, E:]) + nt(d_dt, wdt)
    seq32 = seq.astype(f32)
    scale = lax.rsqrt(jnp.mean(seq32 * seq32, axis=-1, keepdims=True) + EPS)
    unit = seq32 * scale
    g_pre = jnp.sum(d_hidden * unit, axis=0)
    d_unit = d_hidden * pre
    d_seq = scale * (d_unit - unit * jnp.mean(d_unit * unit, axis=-1, keepdims=True))
    d_inputs = to_pieces((cot.astype(f32) + d_seq).astype(bf16), mine)
    g_wdt = tn(hidden, d_dt)[:, :H]
    g_skip_h = g_skip.reshape(H, P_SIZE).sum(axis=1)
    small = jnp.concatenate(
        [
            g_wdt.reshape(2, -1), g_pre.reshape(2, -1),
            g_cw.reshape(K, 2, half).transpose(1, 0, 2).reshape(2, -1), g_cb.reshape(2, -1),
            g_gain.reshape(2, -1), g_bias[0, :H].reshape(2, -1), g_log[0, :H].reshape(2, -1),
            g_skip_h.reshape(2, -1),
        ],
        axis=1,
    )
    small = lax.psum(small, ("rep", "grp"))
    small = lax.dynamic_index_in_dim(small, mine, 0, keepdims=False)
    parts, at = [], 0
    for size in (w_dt.size, pre_gain.size, conv_w.size, half, norm_gain.size, 12, 12, 12):
        parts.append(small[at : at + size])
        at += size
    return (
        result, d_inputs, parts[1], grad_in_w, parts[0].reshape(w_dt.shape),
        parts[2].reshape(K, half), parts[3], parts[5], parts[6], parts[7], parts[4], grad_out_w,
    )


def solution(mesh):
    acts, row, mat, taps = P("rep", "grp", None), P("grp"), P("grp", None), P(None, "grp")
    in_specs = (acts, row, mat, mat, taps, row, row, row, row, row, mat, acts)
    out_specs = (acts, acts, row, mat, mat, taps, row, row, row, row, row, mat)
    return jax.shard_map(
        per_device, mesh=mesh, in_specs=in_specs, out_specs=out_specs, check_vma=False
    )
```

time: 1050 us -> 564 us (0.54)
  matrix products: 276 us -> 41.1 us
  local copies, waits for them, and re-layouts: 179 us -> 21.6 us
  other arithmetic: 142 us -> 19.5 us
  Pallas kernels: 0 us -> 86.3 us
  blocking collectives: 109 us -> 61.4 us
    dot_general x56 -> x7, matrix products: 276 us -> 38.3 us  [the longest x3 19.1 us: tn(): lax.dot_general(a, b, (((0,), (0,)), ((), ())), preferred_element_type=f32)]
    psum x1 -> x2, waiting for transfers between devices: 96 us -> 217 us  [the longest x1 117 us: per_device(): small = lax.psum(small, ('rep', 'grp'))]
    pallas_call x0 -> x2, Pallas kernels: none -> 86.3 us  [the longest x1 47.1 us: backward_call(): pl.pallas_call(backward_kernel, grid=(blocks,), in_specs=[rows(CH), pl.Bl...]
    reduce_scatter x3, waiting for transfers between devices: 106 us -> 32.5 us  [reduced(): lax.psum_scatter(grad.astype(SEND), 'grp', scatter_dimension=0, tiled=True)]
    psum x1 -> x0, blocking collectives: 64.8 us -> none  [per_device(): lax.psum((group_sums[0], group_sums[1], group_sums[2], group_sums[3], gro...]
    reshape x11 -> x12, local copies, waits for them, and re-layouts: 65.2 us -> 2.67 us  [the longest x1 1.25 us: per_device(): g_wdt.reshape(2, -1)]
    unnamed x2 -> x1, blocking collectives: 12.6 us -> 61.4 us
    all_gather x4 -> x2, waiting for transfers between devices: 101 us -> 53.7 us  [per_device(): gather = lambda v, axis=0: lax.all_gather(v, 'grp', axis=axis, tiled=True)]
  transfers between devices with their start and end apart: 11 -> 11, of which waited for: 7 -> 4; matrix products, arithmetic and copies ran while one was open for 25% -> 12% of each run, Pallas kernels for 0% -> 9%
where the time goes in v1:
time: 564 us; the launch traced here: 554 us
  waiting for transfers between devices  304 us (54%)
  Pallas kernels  86.3 us (15%)
  blocking collectives  61.4 us (11%)
  matrix products  41.1 us (7%)
  local copies, waits for them, and re-layouts  21.6 us (4%)
  other arithmetic  19.5 us (3%)
  between operations  15.6 us (3%)
    psum x1, waiting for transfers between devices, per_device(): small = lax.psum(small, ('rep', 'grp'))  117 us
    psum x1, waiting for transfers between devices, reduced(): return lax.psum(part, 'rep').astype(f32)  99.7 us
    unnamed x1, blocking collectives  61.4 us
    all_gather x2, waiting for transfers between devices, per_device(): gather = lambda v, axis=0: lax.all_gather(v, 'grp', axis=axis, tiled=True)  53.7 us
    pallas_call x1, Pallas kernels, backward_call(): pl.pallas_call(backward_kernel, grid=(blocks,), in_specs=[rows(CH), pl.Bl...  47.1 us
    pallas_call x1, Pallas kernels, forward_call(): pl.pallas_call(forward_kernel, grid=(blocks,), in_specs=[rows(width), row...  39.2 us
    reduce_scatter x3, waiting for transfers between devices, reduced(): lax.psum_scatter(grad.astype(SEND), 'grp', scatter_dimension=0, tiled=True)  32.5 us
    dot_general x3, matrix products, tn(): lax.dot_general(a, b, (((0,), (0,)), ((), ())), preferred_element_type=f32)  19.1 us
  transfers between devices with their start and end apart: 11, of which 4 were waited for; matrix products, arithmetic and copies ran while one was open for 12% of the time, Pallas kernels for 9%

profile of v1, /device:TPU:0, one launch (start us, length us, event | category | flops | bytes accessed | tf_op | source)
XLA Modules:
  0.0 554.5 jit_solution(17603130485354951362)
XLA Ops:
  9.8 2.9 collective-permute-start
  16.0 61.4 %all-reduce.3 = bf16[29768]{0:T(1024)(128)(2,1)S(1)} all-reduce(bf16[29768]{0:T(1024)(128)(2,1)S(1)} %dynamic-update-slice), channel_id=2, replica_groups=mesh['rep'=16,'grp'=2] {'grp'}, use_global_device_ids=true, to_apply=%add.3 | all-reduce | flops 29768 | bytes 119072
  83.8 1.4 bitcast_select_fusion.3
  85.3 1.6 bitcast_select_fusion.1
  86.9 1.9 pad_maximum_fusion
  88.8 53.7 %all-gather.4.cloned.1.call-done.w_in_ref = bf16[768,3328]{1,0:T(8,128)(2,1)} async-done(((bf16[384,3328]{1,0:T(8,128)(2,1)}), bf16[768,3328]{1,0:T(8,128)(2,1)}) %all-gather.4.cloned.1.call-update) | async-done | bytes 5111824 | tf_op jit(solution)/shard_map/all_gather | solution.py:374
  142.4 39.2 %mixer_forward.1 = (bf16[1024,768]{1,0:T(8,128)(2,1)}, f32[1024,1792]{1,0:T(8,128)}, f32[1024,128]{1,0:T(8,128)}, bf16[1024,1536]{1,0:T(8,128)(2,1)}, bf16[1024,...) custom-call(bf16[1024,768]{1,0:T(8,128)(2,1)} %get-tuple-element.78., ...), custom_call_target="tpu_custom_call" | custom-call | flops 20000000000 | bytes 40000000 | tf_op jit(solution)/shard_map/mixer_forward/pallas_call | solution.py:280
  181.6 6.4 %convolution_convert_fusion.2 = bf16[768,1536]{1,0:T(8,128)(2,1)} fusion(bf16[1024,768]{1,0:T(8,128)(2,1)} %get-tuple-element.37, bf16[1024,1536]{1,0:T(8,128)(2,1)} %get-tuple-element.29), kind=kOutput, calls=%fused_computation.8 | convolution fusion | flops 2417098752 | bytes 7077888 | tf_op jit(solution)/shard_map/dot_general | solution.py:34
  188.4 6.1 %convolution_convert_fusion = bf16[1536,768]{1,0:T(8,128)(2,1)} fusion(bf16[1024,1536]{1,0:T(8,128)(2,1)} %get-tuple-element.28, bf16[512,768]{1,0:T(8,128)(2,1)S(1)} %get-tuple-element.62, bf16[512,768]{1,0:T(8,128)(2,1)S(1)} %get-tuple-element.61), kind=kOutput, calls=%fused_computation.6 | convolution fusion | flops 2420244480 | bytes 7077888 | tf_op jit(solution)/shard_map/dot_general | solution.py:34
  194.6 47.1 %mixer_backward.1 = (bf16[1024,1792]{1,0:T(8,128)(2,1)}, bf16[1024,128]{1,0:T(8,128)(2,1)}, f32[4,1792]{1,0:T(4,128)}, f32[1,1792]{1,0:T(1,128)}, f32[1,128]{1,0:T(1,128)}, /*index=5*/f32[1,128]{1,0:T(1,128)}) custom-call(f32[1024,1792]{1,0:T(8,128)} %get-tuple-element.30.xbc_ref.before_ref, f32[1024,1792]{1,0:T(8,128)} %get-tuple-element.30.xbc_ref.before_ref, ...), custom_call_target="tpu_custom_call" | custom-call | flops 20000000000 | bytes 30000000 | tf_op jit(solution)/shard_map/mixer_backward/pallas_call | solution.py:312
  241.7 6.6 %convolution_convert_fusion.1 = bf16[768,1792]{1,0:T(8,128)(2,1)} fusion(bf16[1024,768]{1,0:T(8,128)(2,1)S(1)} %copy-done.4, bf16[1024,1792]{1,0:T(8,128)(2,1)} %get-tuple-element.35), kind=kOutput, calls=%fused_computation.7 | convolution fusion | flops 2819948544 | bytes 7995392 | tf_op jit(solution)/shard_map/dot_general | solution.py:34
  248.8 2.8 fusion.15
  252.8 5.5 fusion.13
  258.3 4.9 fusion.11
  263.3 3.6 fusion.8
  268.5 32.5 %reduce-scatter.6.cloned.1.call-done = bf16[384,1792]{1,0:T(8,128)(2,1)} async-done(((bf16[768,1792]{1,0:T(8,128)(2,1)}), bf16[384,1792]{1,0:T(8,128)(2,1)}) %reduce-scatter.6.cloned.1.call-update) | async-done | bytes 1376272 | tf_op jit(solution)/shard_map/reduce_scatter | solution.py:365
  301.0 5.2 fusion.9
  308.7 2.3 fusion.7
  312.1 116.9 %all-reduce.8.cloned.1.call-done = f32[2,14884]{1,0:T(2,128)} async-done(((f32[2,14884]{1,0:T(2,128)}), f32[2,14884]{1,0:T(2,128)}) %all-reduce.8.cloned.1.call-update) | async-done | bytes 119088 | tf_op jit(solution)/shard_map/psum | solution.py:426
  437.8 2.9 maximum_select_fusion
  440.7 1.4 maximum_select_fusion.1
  442.0 99.7 %all-reduce.10.cloned.1.call-done = (bf16[384,1792]{1,0:T(8,128)(2,1)}, bf16[384,1536]{1,0:T(8,128)(2,1)}, bf16[768,768]{1,0:T(8,128)(2,1)}) async-done(((bf16[384,1792]{1,0:T(8,128)(2,1)}, bf16[384,1536]{1,0:T(8,128)(2,1)}, bf16[768,768]{1,0:T(8,128)(2,1)}), (bf16[384,1792]{1,0:T(8,128)(2,1)}, bf16[384,1536]{1,0:T(8,128)(2,1)}, bf16[768,768]{1,0:T(8,128)(2,1)})) %all-reduce.10.cloned.1.call-update) | async-done | bytes 3735568 | tf_op jit(solution)/shard_map/psum | solution.py:366
  541.8 3.0 convert_element_type.117
  544.8 2.6 maximum_convert_fusion
  (135 shorter events, 27.3 us)
Async XLA Ops:
  7.2 5.5 copy-start.3
  7.2 81.6 %all-gather.6.cloned.1.call-start = ((), (), s32[]{:S(2)}) async-start(), calls=%async_computation.4 | async-start | bytes 3538944 | tf_op jit(solution)/shard_map/all_gather | solution.py:374
  7.9 5.7 %copy-start.10 = (bf16[4,896]{1,0:T(4,128)(2,1)S(1)}, bf16[4,896]{1,0:T(4,128)(2,1)}, u32[]{:S(2)}) copy-start(bf16[4,896]{1,0:T(4,128)(2,1)} %param.16) | copy-start | bytes 21508
  7.9 5.7 %copy-start.9 = (bf16[384,24]{0,1:T(8,128)(2,1)S(1)}, bf16[384,24]{0,1:T(8,128)(2,1)}, u32[]{:S(2)}) copy-start(bf16[384,24]{0,1:T(8,128)(2,1)} %param.15) | copy-start | bytes 55300
  8.0 6.0 %copy-start.20 = (u32[32]{0:T(128)S(1)}, u32[32]{0:T(128)}, u32[]{:S(2)}) copy-start(u32[32]{0:T(128)} %constant.71) | copy-start | bytes 388
  8.0 7.3 %copy-start.14 = (bf16[896]{0:T(1024)(128)(2,1)S(1)}, bf16[896]{0:T(1024)(128)(2,1)}, u32[]{:S(2)}) copy-start(bf16[896]{0:T(1024)(128)(2,1)} %param.17) | copy-start | bytes 5380
  8.0 7.3 %copy-start.15 = (bf16[768]{0:T(1024)(128)(2,1)S(1)}, bf16[768]{0:T(1024)(128)(2,1)}, u32[]{:S(2)}) copy-start(bf16[768]{0:T(1024)(128)(2,1)} %param.21) | copy-start | bytes 4612
  8.0 7.3 %copy-start.16 = (bf16[384]{0:T(512)(128)(2,1)S(1)}, bf16[384]{0:T(512)(128)(2,1)}, u32[]{:S(2)}) copy-start(bf16[384]{0:T(512)(128)(2,1)} %param.13) | copy-start | bytes 2308
  8.0 7.3 %copy-start.17 = (bf16[12]{0:T(256)(128)(2,1)S(1)}, bf16[12]{0:T(256)(128)(2,1)}, u32[]{:S(2)}) copy-start(bf16[12]{0:T(256)(128)(2,1)} %param.18) | copy-start | bytes 76
  8.0 7.3 %copy-start.18 = (bf16[12]{0:T(256)(128)(2,1)S(1)}, bf16[12]{0:T(256)(128)(2,1)}, u32[]{:S(2)}) copy-start(bf16[12]{0:T(256)(128)(2,1)} %param.19) | copy-start | bytes 76
  8.0 7.3 %copy-start.19 = (bf16[12]{0:T(256)(128)(2,1)S(1)}, bf16[12]{0:T(256)(128)(2,1)}, u32[]{:S(2)}) copy-start(bf16[12]{0:T(256)(128)(2,1)} %param.20) | copy-start | bytes 76
  8.0 134.4 %all-gather.4.cloned.1.call-start = ((), (), s32[]{:S(2)}) async-start(), calls=%async_computation.3 | async-start | bytes 7667712 | tf_op jit(solution)/shard_map/all_gather | solution.py:374
  8.8 259.7 %reduce-scatter.4.cloned.1.call-start = ((), (), s32[]{:S(2)}) async-start(), calls=%async_computation.6 | async-start | bytes 3538944 | tf_op jit(solution)/shard_map/reduce_scatter | solution.py:365
  9.8 74.1 %collective-permute-start = (bf16[512,768]{1,0:T(8,128)(2,1)}, bf16[512,768]{1,0:T(8,128)(2,1)}, u32[]{:S(2)}, u32[]{:S(2)}) collective-permute-start(bf16[512,768]{1,0:T(8,128)(2,1)} %dynamic-slice_bitcast_fusion.3), channel_id=1, source_target_pairs={{0,1},{1,0},{2,3},{3,2},{4,5},{5,4},{6,7},{7,6},{8,9},{9,8},{10,11... | collective-permute-start | bytes 2359304 | tf_op jit(solution)/shard_map/ppermute | solution.py:347
  13.7 71.6 %collective-permute-start.1 = (bf16[512,768]{1,0:T(8,128)(2,1)}, bf16[512,768]{1,0:T(8,128)(2,1)}, u32[]{:S(2)}, u32[]{:S(2)}) collective-permute-start(bf16[512,768]{1,0:T(8,128)(2,1)} %dynamic-slice_bitcast_fusion.2), channel_id=1, source_target_pairs={{0,1},{1,0},{2,3},{3,2},{4,5},{5,4},{6,7},{7,6},{8,9},{9,8},{10,11... | collective-permute-start | bytes 2359304 | tf_op jit(solution)/shard_map/ppermute | solution.py:347
  188.0 80.5 %reduce-scatter.8.cloned.1.call-start = ((), (), s32[]{:S(2)}) async-start(), calls=%async_computation.8 | async-start | bytes 3538944 | tf_op jit(solution)/shard_map/reduce_scatter | solution.py:365
  194.5 106.5 %reduce-scatter.6.cloned.1.call-start = ((), (), s32[]{:S(2)}) async-start(), calls=%async_computation.7 | async-start | bytes 4128768 | tf_op jit(solution)/shard_map/reduce_scatter | solution.py:365
  194.6 47.2 %copy-start.4 = (bf16[1024,768]{1,0:T(8,128)(2,1)S(1)}, bf16[1024,768]{1,0:T(8,128)(2,1)}, u32[]{:S(2)}) copy-start(bf16[1024,768]{1,0:T(8,128)(2,1)} %get-tuple-element.37) | copy-start | bytes 4718596
  248.3 180.6 %all-reduce.8.cloned.1.call-start = ((), (), s32[]{:S(2)}) async-start(), calls=%async_computation.5 | async-start | bytes 239616 | tf_op jit(solution)/shard_map/psum | solution.py:426
  252.8 5.5 copy-start.23
  268.4 273.3 %all-reduce.10.cloned.1.call-start = ((), (), s32[]{:S(2)}) async-start(), calls=%async_computation.9 | async-start | bytes 7471104 | tf_op jit(solution)/shard_map/psum | solution.py:366
  307.5 130.3 %collective-permute-start.2 = (bf16[512,768]{1,0:T(8,128)(2,1)}, bf16[512,768]{1,0:T(8,128)(2,1)}, u32[]{:S(2)}, u32[]{:S(2)}) collective-permute-start(bf16[512,768]{1,0:T(8,128)(2,1)} %get-tuple-element.68), channel_id=1, source_target_pairs={{0,1},{1,0},{2,3},{3,2},{4,5},{5,4},{6,7},{7,6},{8,9},{9,8},{10,11... | collective-permute-start | bytes 2359304 | tf_op jit(solution)/shard_map/ppermute | solution.py:356
  311.0 126.7 %copy-start.1 = (bf16[1,512,768]{2,1,0:T(8,128)(2,1)S(1)}, bf16[1,512,768]{2,1,0:T(8,128)(2,1)}, u32[]{:S(2)}) copy-start(bf16[1,512,768]{2,1,0:T(8,128)(2,1)} %get-tuple-element.67) | copy-start | bytes 2359300
  311.2 129.5 %collective-permute-start.3 = (bf16[512,768]{1,0:T(8,128)(2,1)S(1)}, bf16[512,768]{1,0:T(8,128)(2,1)S(1)}, u32[]{:S(2)}, u32[]{:S(2)}) collective-permute-start(bf16[512,768]{1,0:T(8,128)(2,1)S(1)} %get-tuple-element.66), channel_id=1, source_target_pairs={{0,1},{1,0},{2,3},{3,2},{4,5},{5,4},{6,7},{7,6},{8,9},{9,8},{10,11... | collective-permute-start | bytes 2359304 | tf_op jit(solution)/shard_map/ppermute | solution.py:356
  (11 other events, 38.1 us)
Sparse Core Ops, SparseCore 0:
  9.6 63.6 all-gather.5
  74.8 67.5 all-gather.3
  188.2 34.7 reduce-scatter.3
  225.1 34.6 reduce-scatter.7
  261.9 39.0 reduce-scatter.5
  307.3 121.5 all-reduce.7
  433.4 108.3 all-reduce.9

commit v2 on v1

--- a/solution.py
+++ b/solution.py
@@ -361,9 +361,56 @@
     return jnp.pad(v, [(0, 0)] * (v.ndim - 1) + [(0, PAD - H)])
 
 
-def reduced(grad):
-    part = lax.psum_scatter(grad.astype(SEND), "grp", scatter_dimension=0, tiled=True)
-    return lax.psum(part, "rep").astype(f32)
+def flipped(v, bit):
+    size = lax.axis_size("rep")
+    return lax.ppermute(v, "rep", [(i, i ^ (1 << bit)) for i in range(size)])
+
+
+def bit_of(bit):
+    return (lax.axis_index("rep") >> bit) & 1
+
+
+def in_order(kept, other, high, axis=0):
+    first = jnp.where(high == 0, kept, other)
+    second = jnp.where(high == 0, other, kept)
+    return jnp.concatenate([first, second], axis=axis)
+
+
+def gathered_rows(shard, mine):
+    rows, columns = shard.shape
+    quarter = rows // 4
+    place = lax.axis_index("rep") & 3
+    part = lax.dynamic_slice_in_dim(shard, place * quarter, quarter, axis=0)
+    part = lax.ppermute(part, "grp", SWAP)[None, None]
+    part = in_order(part, flipped(part, 1), bit_of(1), axis=0)
+    part = in_order(part, flipped(part, 0), bit_of(0), axis=1)
+    return in_order(shard, part.reshape(rows, columns), mine)
+
+
+def summed_over_all(halves, mine):
+    kept = lax.dynamic_index_in_dim(halves, mine, 0, keepdims=False)
+    sent = lax.dynamic_index_in_dim(halves, 1 - mine, 0, keepdims=False).astype(SEND)
+    total = kept + lax.ppermute(sent, "grp", SWAP).astype(f32)
+    bits = (lax.axis_size("rep") - 1).bit_length()
+    for bit in range(bits):
+        half = total.shape[0] // 2
+        high = bit_of(bit)
+        kept = lax.dynamic_slice_in_dim(total, high * half, half, axis=0)
+        sent = lax.dynamic_slice_in_dim(total, (1 - high) * half, half, axis=0).astype(SEND)
+        total = kept + flipped(sent, bit).astype(f32)
+    total = total.astype(SEND)
+    for bit in reversed(range(bits)):
+        total = in_order(total, flipped(total, bit), bit_of(bit))
+    return total.astype(f32)
+
+
+def summed_small(halves, mine):
+    kept = lax.dynamic_index_in_dim(halves, mine, 0, keepdims=False)
+    sent = lax.dynamic_index_in_dim(halves, 1 - mine, 0, keepdims=False)
+    total = kept + lax.ppermute(sent, "grp", SWAP)
+    for bit in range((lax.axis_size("rep") - 1).bit_length()):
+        total = total + flipped(total, bit)
+    return total
 
 
 def per_device(
@@ -371,11 +418,10 @@
     cotangent,
 ):
     mine = lax.axis_index("grp")
-    gather = lambda v, axis=0: lax.all_gather(v, "grp", axis=axis, tiled=True)
     vectors = jnp.concatenate(
         [conv_w.reshape(-1), pre_gain, conv_b, dt_bias, a_log, d_skip, norm_gain, w_dt.reshape(-1)]
     )
-    both = lax.all_gather(vectors, "grp", axis=0)
+    both = in_order(vectors[None], lax.ppermute(vectors[None], "grp", SWAP), mine)
     sizes = [conv_w.size, pre_gain.size, conv_b.size, H // 2, H // 2, H // 2, norm_gain.size]
     cuts, at = [], 0
     for size in sizes:
@@ -387,8 +433,8 @@
     wdt = pad_heads(both[:, at:].reshape(-1, H))
     bias, log_rate = pad_heads(bias), pad_heads(log_rate)
     skip = jnp.repeat(skip, P_SIZE, axis=1)
-    win = gather(w_in)
-    wout = gather(w_out)
+    win = gathered_rows(w_in, mine)
+    wout = gathered_rows(w_out, mine)
     heads = (jnp.arange(PAD)[:, None] == jnp.arange(E)[None, :] // P_SIZE).astype(bf16)
     heads2 = jnp.concatenate([heads, heads], axis=0)
     seq = to_sequence(inputs, mine)
@@ -396,13 +442,18 @@
     hidden, xbc, dt, normed, d_gate, dy, r1, starts, g_gain, g_skip = forward_call(
         seq, cot, pre, win, wdt, cw, cb, bias, log_rate, skip, gain, wout, heads2
     )
-    grad_out_w = reduced(tn(normed, cot))
-    grad_gate_w = reduced(tn(hidden, d_gate))
+    g_out = tn(normed, cot).reshape(2, E // 2, -1)
+    g_gate = tn(hidden, d_gate).reshape(2, -1, E)
+    early = jnp.concatenate([g_out, g_gate[:, :, : E // 2], g_gate[:, :, E // 2 :]], axis=1)
+    early = summed_over_all(early, mine)
+    third = w_in.shape[0]
+    grad_out_w = early[: E // 2]
+    grad_gate_w = jnp.concatenate([early[E // 2 : E // 2 + third], early[E // 2 + third :]], axis=1)
     result = to_pieces((seq.astype(f32) + nn(normed, wout)).astype(bf16), mine)
     d_xbc, d_dt, g_cw, g_cb, g_bias, g_log = backward_call(
         xbc, dt, dy, r1, starts, cw, cb, bias, log_rate, skip, heads2
     )
-    grad_xbc_w = reduced(tn(hidden, d_xbc))
+    grad_xbc_w = summed_over_all(tn(hidden, d_xbc).reshape(2, -1, CH), mine)
     grad_in_w = jnp.concatenate([grad_gate_w, grad_xbc_w], axis=1)
     d_hidden = nt(d_gate, win[:, :E]) + nt(d_xbc, win[:, E:]) + nt(d_dt, wdt)
     seq32 = seq.astype(f32)
@@ -423,8 +474,7 @@
         ],
         axis=1,
     )
-    small = lax.psum(small, ("rep", "grp"))
-    small = lax.dynamic_index_in_dim(small, mine, 0, keepdims=False)
+    small = summed_small(small, mine)
     parts, at = [], 0
     for size in (w_dt.size, pre_gain.size, conv_w.size, half, norm_gain.size, 12, 12, 12):
         parts.append(small[at : at + size])

time: 564 us -> 401 us (0.71)
  waiting for transfers between devices: 304 us -> 132 us
  blocking collectives: 61.4 us -> 0 us
  starting transfers between devices: 4.84 us -> 43.4 us
  other arithmetic: 19.5 us -> 48.6 us
  local copies, waits for them, and re-layouts: 21.6 us -> 45.3 us
  between operations: 15.6 us -> 1.69 us
    psum x2 -> x0, waiting for transfers between devices: 217 us -> none  [the longest x1 117 us: per_device(): small = lax.psum(small, ('rep', 'grp'))]
    ppermute x0 -> x30, waiting for transfers between devices: none -> 102 us  [the longest x2 50.6 us: summed_over_all(): total = kept + lax.ppermute(sent, 'grp', SWAP).astype(f32)]
    unnamed x1 -> x0, blocking collectives: 61.4 us -> none
    all_gather x2 -> x0, waiting for transfers between devices: 53.7 us -> none  [per_device(): gather = lambda v, axis=0: lax.all_gather(v, 'grp', axis=axis, tiled=True)]
    ppermute x0 -> x30, starting transfers between devices: none -> 39.4 us  [the longest x24 31.3 us: flipped(): return lax.ppermute(v, 'rep', [(i, i ^ 1 << bit) for i in range(size)])]
    reduce_scatter x3 -> x0, waiting for transfers between devices: 32.5 us -> none  [reduced(): lax.psum_scatter(grad.astype(SEND), 'grp', scatter_dimension=0, tiled=True)]
    ppermute x2, waiting for transfers between devices: 0.01 us -> 30.7 us  [to_sequence(): lax.ppermute(lax.dynamic_index_in_dim(pieces, 1 - mine, 0, keepdims=False...]
    concatenate x0 -> x15, other arithmetic: none -> 15.4 us  [the longest x1 8.03 us: per_device(): jnp.concatenate([g_out, g_gate[:, :, :E // 2], g_gate[:, :, E // 2:]], ax...]
  transfers between devices with their start and end apart: 11 -> 34, of which waited for: 4 -> 17; matrix products, arithmetic and copies ran while one was open for 12% -> 18% of each run, Pallas kernels for 9% -> 0%
where the time goes in v2:
time: 401 us; the launch traced here: 395 us
  waiting for transfers between devices  132 us (33%)
  Pallas kernels  87 us (22%)
  other arithmetic  48.6 us (12%)
  local copies, waits for them, and re-layouts  45.3 us (11%)
  starting transfers between devices  43.4 us (11%)
  matrix products  36.7 us (9%)
    ppermute x2, waiting for transfers between devices, summed_over_all(): total = kept + lax.ppermute(sent, 'grp', SWAP).astype(f32)  50.6 us
    pallas_call x1, Pallas kernels, backward_call(): pl.pallas_call(backward_kernel, grid=(blocks,), in_specs=[rows(CH), pl.Bl...  47.7 us
    ppermute x24, waiting for transfers between devices, flipped(): return lax.ppermute(v, 'rep', [(i, i ^ 1 << bit) for i in range(size)])  43.9 us
    pallas_call x1, Pallas kernels, forward_call(): pl.pallas_call(forward_kernel, grid=(blocks,), in_specs=[rows(width), row...  39.3 us
    ppermute x24, starting transfers between devices, flipped(): return lax.ppermute(v, 'rep', [(i, i ^ 1 << bit) for i in range(size)])  31.3 us
    ppermute x2, waiting for transfers between devices, to_sequence(): lax.ppermute(lax.dynamic_index_in_dim(pieces, 1 - mine, 0, keepdims=False...  30.7 us
    dot_general x3, matrix products, nt(): lax.dot_general(a, b, (((1,), (1,)), ((), ())), preferred_element_type=f32)  17.9 us
    dot_general x3, matrix products, tn(): lax.dot_general(a, b, (((0,), (0,)), ((), ())), preferred_element_type=f32)  15.6 us
  transfers between devices with their start and end apart: 34, of which 17 were waited for; matrix products, arithmetic and copies ran while one was open for 18% of the time, Pallas kernels for 0%

profile of v2, /device:TPU:0, one launch (start us, length us, event | category | flops | bytes accessed | tf_op | source)
XLA Modules:
  0.0 395.1 jit_solution(4338002151412368498)
XLA Ops:
  2.6 4.2 %concatenate.70 = bf16[14884]{0:T(1024)(128)(2,1)S(1)} concatenate(bf16[3584]{0:T(1024)(128)(2,1)S(1)} %reshape.231, bf16[384]{0:T(512)(128)(2,1)} %param.13, bf16[896]{0:T(1024)(128)(2,1)} %param.17, bf16[12]{0:T(256)(128)(2,1)} %param.18, bf16[12]{0:T(256)(128)(2,1)} %param.19, bf16[12]{0:T(256)(128)(2,1)} %param.20, bf16[768]{0:T(1024)(128)(2,1)} %param.21, ...), dimensions={0} | concatenate | bytes 59536 | tf_op jit(solution)/shard_map/concatenate | solution.py:421
  29.5 5.6 %collective-permute-done.3 = bf16[96,3328]{1,0:T(8,128)(2,1)} collective-permute-done((bf16[96,3328]{1,0:T(8,128)(2,1)}, bf16[96,3328]{1,0:T(8,128)(2,1)}, u32[]{:S(2)}, u32[]{:S(2)}) %collective-permute-start.3) | collective-permute-done | bytes 639008 | tf_op jit(solution)/shard_map/ppermute | solution.py:384
  36.7 30.7 %collective-permute-done = bf16[512,768]{1,0:T(8,128)(2,1)} collective-permute-done((bf16[512,768]{1,0:T(8,128)(2,1)S(1)}, bf16[512,768]{1,0:T(8,128)(2,1)}, u32[]{:S(2)}, u32[]{:S(2)}) %collective-permute-start) | collective-permute-done | bytes 786464 | tf_op jit(solution)/shard_map/ppermute | solution.py:347
  83.5 39.3 %mixer_forward.1 = (bf16[1024,768]{1,0:T(8,128)(2,1)}, f32[1024,1792]{1,0:T(8,128)}, f32[1024,128]{1,0:T(8,128)}, bf16[1024,1536]{1,0:T(8,128)(2,1)}, bf16[1024,...) custom-call(bf16[1024,768]{1,0:T(8,128)(2,1)} %get-tuple-element.109, ...), custom_call_target="tpu_custom_call" | custom-call | flops 20000000000 | bytes 40000000 | tf_op jit(solution)/shard_map/mixer_forward/pallas_call | solution.py:280
  122.8 47.7 %mixer_backward.1 = (bf16[1024,1792]{1,0:T(8,128)(2,1)}, bf16[1024,128]{1,0:T(8,128)(2,1)}, f32[4,1792]{1,0:T(4,128)}, f32[1,1792]{1,0:T(1,128)}, f32[1,128]{1,0:T(1,128)}, /*index=5*/f32[1,128]{1,0:T(1,128)}) custom-call(f32[1024,1792]{1,0:T(8,128)} %get-tuple-element.30.xbc_ref.before_ref, f32[1024,1792]{1,0:T(8,128)} %get-tuple-element.30.xbc_ref.before_ref, ...), custom_call_target="tpu_custom_call" | custom-call | flops 20000000000 | bytes 30000000 | tf_op jit(solution)/shard_map/mixer_backward/pallas_call | solution.py:312
  170.5 3.3 fusion.29
  174.5 6.9 %fusion.12 = f32[1024,768]{1,0:T(8,128)} fusion(bf16[1024,1792]{1,0:T(8,128)(2,1)} %get-tuple-element.35, bf16[384,3328]{1,0:T(8,128)(2,1)S(1)} %get-tuple-element.60, bf16[384,3328]{1,0:T(8,128)(2,1)S(1)} %copy-done.4), kind=kOutput, calls=%fused_computation.25 | convolution fusion | flops 2824077312 | bytes 11927552 | tf_op jit(solution)/shard_map/dot_general | solution.py:30
  181.4 4.8 %fusion.36 = f32[768,1792]{1,0:T(8,128)} fusion(bf16[1024,768]{1,0:T(8,128)(2,1)S(1)} %copy-done, bf16[1024,1792]{1,0:T(8,128)(2,1)S(1)} %copy-done.15), kind=kOutput, calls=%fused_computation.148 | convolution fusion | flops 2818572288 | bytes 10747904 | tf_op jit(solution)/shard_map/dot_general | solution.py:34
  195.9 6.3 %fusion.35 = f32[768,1536]{1,0:T(8,128)} fusion(bf16[1024,768]{1,0:T(8,128)(2,1)S(1)} %copy-done, bf16[1024,1536]{1,0:T(8,128)(2,1)} %get-tuple-element.29), kind=kOutput, calls=%fused_computation.147 | convolution fusion | flops 2415919104 | bytes 9437184 | tf_op jit(solution)/shard_map/dot_general | solution.py:34
  202.3 7.7 %fusion.8 = (f32[768]{0:T(1024)S(1)}, f32[1024]{0:T(1024)S(1)}, f32[1024,768]{1,0:T(8,128)}) fusion(f32[1024]{0:T(1024)S(1)} %copy-done.28, bf16[512,768]{1,0:T(8,128)(2,1)S(1)} %get-tuple-element.75, bf16[512,768]{1,0:T(8,128)(2,1)S(1)} %get-tuple-element.74, f32[768]{0:T(1024)S(1)} %reshape.256, f32[1024,768]{1,0:T(8,128)S(1)} %copy-done.17, ...), kind=kOutput, calls=%fused_computation.20 | convolution fusion | flops 2430073088 | bytes 19281920 | tf_op jit(solution)/shard_map/dot_general | solution.py:30
  211.5 5.0 %fusion.32 = (f32[2,384,768]{2,1,0:T(8,128)}, f32[2,384,768]{2,1,0:T(8,128)}) fusion(f32[2,384,1536]{2,1,0:T(8,128)} %bitcast.74), kind=kLoop, calls=%fused_computation.144 | loop fusion | bytes 9437184 | tf_op jit(solution)/shard_map/slice | solution.py:447
  216.6 3.1 fusion.20
  220.8 4.5 %fusion.31 = f32[1536,768]{1,0:T(8,128)} fusion(bf16[1024,1536]{1,0:T(8,128)(2,1)S(1)} %copy-done.33, bf16[512,768]{1,0:T(8,128)(2,1)S(1)} %copy-done.9, bf16[512,768]{1,0:T(8,128)(2,1)S(1)} %copy-done.7), kind=kOutput, calls=%fused_computation.143 | convolution fusion | flops 2419064832 | bytes 9437184 | tf_op jit(solution)/shard_map/dot_general | solution.py:34
  225.3 8.0 %pad_maximum_fusion = f32[2,1536,768]{2,1,0:T(8,128)} fusion(f32[2,384,768]{2,1,0:T(8,128)} %get-tuple-element.63, f32[2,384,768]{2,1,0:T(8,128)} %get-tuple-element.62, f32[2,768,768]{2,1,0:T(8,128)} %bitcast.78), kind=kLoop, calls=%fused_computation | loop fusion | flops 4718592 | bytes 18874368 | tf_op jit(solution)/shard_map/concatenate | solution.py:447
  236.9 16.1 %collective-permute-done.25 = bf16[384,1792]{1,0:T(8,128)(2,1)} collective-permute-done((bf16[384,1792]{1,0:T(8,128)(2,1)}, bf16[384,1792]{1,0:T(8,128)(2,1)}, u32[]{:S(2)}, u32[]{:S(2)}) %collective-permute-start.25) | collective-permute-done | bytes 1376288 | tf_op jit(solution)/shard_map/ppermute | solution.py:393
  268.9 34.5 %collective-permute-done.16 = bf16[1536,768]{1,0:T(8,128)(2,1)S(1)} collective-permute-done((bf16[1536,768]{1,0:T(8,128)(2,1)S(1)}, bf16[1536,768]{1,0:T(8,128)(2,1)S(1)}, u32[]{:S(2)}, u32[]{:S(2)}) %collective-permute-start.16) | collective-permute-done | bytes 2359328 | tf_op jit(solution)/shard_map/ppermute | solution.py:393
  321.4 6.9 %collective-permute-done.18 = bf16[384,768]{1,0:T(8,128)(2,1)S(1)} collective-permute-done((bf16[384,768]{1,0:T(8,128)(2,1)S(1)}, bf16[384,768]{1,0:T(8,128)(2,1)S(1)}, u32[]{:S(2)}, u32[]{:S(2)}) %collective-permute-start.18) | collective-permute-done | bytes 589856 | tf_op jit(solution)/shard_map/ppermute | solution.py:366
  332.0 4.4 %collective-permute-done.19 = bf16[192,768]{1,0:T(8,128)(2,1)S(1)} collective-permute-done((bf16[192,768]{1,0:T(8,128)(2,1)S(1)}, bf16[192,768]{1,0:T(8,128)(2,1)S(1)}, u32[]{:S(2)}, u32[]{:S(2)}) %collective-permute-start.19) | collective-permute-done | bytes 294944 | tf_op jit(solution)/shard_map/ppermute | solution.py:366
  336.5 3.7 collective-permute-start.20
  340.2 6.6 %collective-permute-done.20 = bf16[96,768]{1,0:T(8,128)(2,1)S(1)} collective-permute-done((bf16[96,768]{1,0:T(8,128)(2,1)S(1)}, bf16[96,768]{1,0:T(8,128)(2,1)S(1)}, u32[]{:S(2)}, u32[]{:S(2)}) %collective-permute-start.20) | collective-permute-done | bytes 147488 | tf_op jit(solution)/shard_map/ppermute | solution.py:366
  349.9 4.4 %collective-permute-done.21 = bf16[96,768]{1,0:T(8,128)(2,1)S(1)} collective-permute-done((bf16[96,768]{1,0:T(8,128)(2,1)S(1)}, bf16[96,768]{1,0:T(8,128)(2,1)S(1)}, u32[]{:S(2)}, u32[]{:S(2)}) %collective-permute-start.21) | collective-permute-done | bytes 147488 | tf_op jit(solution)/shard_map/ppermute | solution.py:366
  358.0 3.3 collective-permute-done.22
  363.0 4.5 %collective-permute-done.32 = bf16[96,1792]{1,0:T(8,128)(2,1)S(1)} collective-permute-done((bf16[96,1792]{1,0:T(8,128)(2,1)S(1)}, bf16[96,1792]{1,0:T(8,128)(2,1)S(1)}, u32[]{:S(2)}, u32[]{:S(2)}) %collective-permute-start.32) | collective-permute-done | bytes 344096 | tf_op jit(solution)/shard_map/ppermute | solution.py:366
  368.4 6.6 %collective-permute-done.23 = bf16[384,768]{1,0:T(8,128)(2,1)S(1)} collective-permute-done((bf16[384,768]{1,0:T(8,128)(2,1)S(1)}, bf16[384,768]{1,0:T(8,128)(2,1)S(1)}, u32[]{:S(2)}, u32[]{:S(2)}) %collective-permute-start.23) | collective-permute-done | bytes 589856 | tf_op jit(solution)/shard_map/ppermute | solution.py:366
  (259 shorter events, 125.4 us)
Async XLA Ops:
  7.4 12.1 %collective-permute-start.2 = (bf16[1,14884]{1,0:T(2,128)(2,1)}, bf16[1,14884]{1,0:T(2,128)(2,1)S(1)}, u32[]{:S(2)}, u32[]{:S(2)}) collective-permute-start(bf16[1,14884]{1,0:T(2,128)(2,1)} %broadcast_in_dim.19), channel_id=1, source_target_pairs={{0,1},{1,0},{2,3},{3,2},{4,5},{5,4},{6,7},{7,6},{8,9},{9,8},{10,11... | collective-permute-start | bytes 89312 | tf_op jit(solution)/shard_map/ppermute | solution.py:424
  11.4 10.1 %collective-permute-start.6 = (bf16[192,768]{1,0:T(8,128)(2,1)S(1)}, bf16[192,768]{1,0:T(8,128)(2,1)}, u32[]{:S(2)}, u32[]{:S(2)}) collective-permute-start(bf16[192,768]{1,0:T(8,128)(2,1)S(1)} %constant_dynamic-slice_fusion.2), channel_id=1, source_target_pairs={{0,1},{1,0},{2,3},{3,2},{4,5},{5,4},{6,7},{7,6},{8,9},{9,8},{10,11... | collective-permute-start | bytes 884744 | tf_op jit(solution)/shard_map/ppermute | solution.py:384
  13.4 21.8 %collective-permute-start.3 = (bf16[96,3328]{1,0:T(8,128)(2,1)}, bf16[96,3328]{1,0:T(8,128)(2,1)}, u32[]{:S(2)}, u32[]{:S(2)}) collective-permute-start(bf16[96,3328]{1,0:T(8,128)(2,1)} %constant_dynamic-slice_fusion.3), channel_id=1, source_target_pairs={{0,1},{1,0},{2,3},{3,2},{4,5},{5,4},{6,7},{7,6},{8,9},{9,8},{10,11... | collective-permute-start | bytes 1916936 | tf_op jit(solution)/shard_map/ppermute | solution.py:384
  16.3 52.7 %collective-permute-start.1 = (bf16[512,768]{1,0:T(8,128)(2,1)}, bf16[512,768]{1,0:T(8,128)(2,1)}, u32[]{:S(2)}, u32[]{:S(2)}) collective-permute-start(bf16[512,768]{1,0:T(8,128)(2,1)} %dynamic-slice_bitcast_fusion.2), channel_id=1, source_target_pairs={{0,1},{1,0},{2,3},{3,2},{4,5},{5,4},{6,7},{7,6},{8,9},{9,8},{10,11... | collective-permute-start | bytes 2359304 | tf_op jit(solution)/shard_map/ppermute | solution.py:347
  16.4 51.0 %collective-permute-start = (bf16[512,768]{1,0:T(8,128)(2,1)S(1)}, bf16[512,768]{1,0:T(8,128)(2,1)}, u32[]{:S(2)}, u32[]{:S(2)}) collective-permute-start(bf16[512,768]{1,0:T(8,128)(2,1)S(1)} %dynamic-slice_bitcast_fusion.3), channel_id=1, source_target_pairs={{0,1},{1,0},{2,3},{3,2},{4,5},{5,4},{6,7},{7,6},{8,9},{9,8},{10,11... | collective-permute-start | bytes 2359304 | tf_op jit(solution)/shard_map/ppermute | solution.py:347
  29.5 45.0 %collective-permute-start.8 = (bf16[2,1,192,768]{3,2,1,0:T(8,128)(2,1)S(1)}, bf16[2,1,192,768]{3,2,1,0:T(8,128)(2,1)S(1)}, u32[]{:S(2)}, u32[]{:S(2)}) collective-permute-start(bf16[2,1,192,768]{3,2,1,0:T(8,128)(2,1)S(1)} %pad_maximum_fusion.12), channel_id=1, source_target_pairs={{0,2},{2,0},{4,6},{6,4},{8,10},{10,8},{12,14},{14,12},{16,18},{18,... | collective-permute-start | bytes 1769480 | tf_op jit(solution)/shard_map/ppermute | solution.py:366
  35.2 37.3 %collective-permute-start.4 = (bf16[1,1,96,3328]{3,2,1,0:T(8,128)(2,1)}, bf16[1,1,96,3328]{3,2,1,0:T(8,128)(2,1)S(1)}, u32[]{:S(2)}, u32[]{:S(2)}) collective-permute-start(bf16[1,1,96,3328]{3,2,1,0:T(8,128)(2,1)} %bitcast.4), channel_id=1, source_target_pairs={{0,4},{2,6},{4,0},{6,2},{8,12},{10,14},{12,8},{14,10},{16,20},{18,... | collective-permute-start | bytes 1916936 | tf_op jit(solution)/shard_map/ppermute | solution.py:366
  210.5 47.7 %collective-permute-start.11 = (f32[14884]{0:T(1024)S(1)}, f32[14884]{0:T(1024)S(1)}, u32[]{:S(2)}, u32[]{:S(2)}) collective-permute-start(f32[14884]{0:T(1024)S(1)} %get-tuple-element.58), channel_id=1, source_target_pairs={{0,1},{1,0},{2,3},{3,2},{4,5},{5,4},{6,7},{7,6},{8,9},{9,8},{10,11... | collective-permute-start | bytes 178616 | tf_op jit(solution)/shard_map/ppermute | solution.py:410
  219.7 33.3 %collective-permute-start.25 = (bf16[384,1792]{1,0:T(8,128)(2,1)}, bf16[384,1792]{1,0:T(8,128)(2,1)}, u32[]{:S(2)}, u32[]{:S(2)}) collective-permute-start(bf16[384,1792]{1,0:T(8,128)(2,1)} %fusion.20), channel_id=1, source_target_pairs={{0,1},{1,0},{2,3},{3,2},{4,5},{5,4},{6,7},{7,6},{8,9},{9,8},{10,11... | collective-permute-start | bytes 4128776 | tf_op jit(solution)/shard_map/ppermute | solution.py:393
  235.9 67.6 %collective-permute-start.16 = (bf16[1536,768]{1,0:T(8,128)(2,1)S(1)}, bf16[1536,768]{1,0:T(8,128)(2,1)S(1)}, u32[]{:S(2)}, u32[]{:S(2)}) collective-permute-start(bf16[1536,768]{1,0:T(8,128)(2,1)S(1)} %fusion.14), channel_id=1, source_target_pairs={{0,1},{1,0},{2,3},{3,2},{4,5},{5,4},{6,7},{7,6},{8,9},{9,8},{10,11... | collective-permute-start | bytes 7077896 | tf_op jit(solution)/shard_map/ppermute | solution.py:393
  255.5 11.6 %collective-permute-start.26 = (bf16[192,1792]{1,0:T(8,128)(2,1)S(1)}, bf16[192,1792]{1,0:T(8,128)(2,1)S(1)}, u32[]{:S(2)}, u32[]{:S(2)}) collective-permute-start(bf16[192,1792]{1,0:T(8,128)(2,1)S(1)} %dynamic-slice_convert_fusion.3), channel_id=1, source_target_pairs={{0,2},{2,0},{4,6},{6,4},{8,10},{10,8},{12,14},{14,12},{16,18},{18,... | collective-permute-start | bytes 2064392 | tf_op jit(solution)/shard_map/ppermute | solution.py:366
  260.1 121.7 %collective-permute-start.9 = (bf16[512,768]{1,0:T(8,128)(2,1)}, bf16[512,768]{1,0:T(8,128)(2,1)}, u32[]{:S(2)}, u32[]{:S(2)}) collective-permute-start(bf16[512,768]{1,0:T(8,128)(2,1)} %get-tuple-element.79), channel_id=1, source_target_pairs={{0,1},{1,0},{2,3},{3,2},{4,5},{5,4},{6,7},{7,6},{8,9},{9,8},{10,11... | collective-permute-start | bytes 2359304 | tf_op jit(solution)/shard_map/ppermute | solution.py:356
  265.5 42.0 %collective-permute-start.14 = (f32[14884]{0:T(1024)S(1)}, f32[14884]{0:T(1024)S(1)}, u32[]{:S(2)}, u32[]{:S(2)}) collective-permute-start(f32[14884]{0:T(1024)S(1)} %add.169), channel_id=1, source_target_pairs={{0,8},{2,10},{4,12},{6,14},{8,0},{10,2},{12,4},{14,6},{16,24},{18,... | collective-permute-start | bytes 178616 | tf_op jit(solution)/shard_map/ppermute | solution.py:366
  267.3 45.6 %collective-permute-start.27 = (bf16[96,1792]{1,0:T(8,128)(2,1)S(1)}, bf16[96,1792]{1,0:T(8,128)(2,1)S(1)}, u32[]{:S(2)}, u32[]{:S(2)}) collective-permute-start(bf16[96,1792]{1,0:T(8,128)(2,1)S(1)} %dynamic-slice_convert_fusion.5), channel_id=1, source_target_pairs={{0,4},{2,6},{4,0},{6,2},{8,12},{10,14},{12,8},{14,10},{16,20},{18,... | collective-permute-start | bytes 1032200 | tf_op jit(solution)/shard_map/ppermute | solution.py:366
  304.1 10.7 %collective-permute-start.17 = (bf16[768,768]{1,0:T(8,128)(2,1)S(1)}, bf16[768,768]{1,0:T(8,128)(2,1)S(1)}, u32[]{:S(2)}, u32[]{:S(2)}) collective-permute-start(bf16[768,768]{1,0:T(8,128)(2,1)S(1)} %dynamic-slice_convert_fusion.2), channel_id=1, source_target_pairs={{0,2},{2,0},{4,6},{6,4},{8,10},{10,8},{12,14},{14,12},{16,18},{18,... | collective-permute-start | bytes 3538952 | tf_op jit(solution)/shard_map/ppermute | solution.py:366
  311.4 73.2 %collective-permute-start.10 = (bf16[512,768]{1,0:T(8,128)(2,1)}, bf16[512,768]{1,0:T(8,128)(2,1)}, u32[]{:S(2)}, u32[]{:S(2)}) collective-permute-start(bf16[512,768]{1,0:T(8,128)(2,1)} %get-tuple-element.77), channel_id=1, source_target_pairs={{0,1},{1,0},{2,3},{3,2},{4,5},{5,4},{6,7},{7,6},{8,9},{9,8},{10,11... | collective-permute-start | bytes 2359304 | tf_op jit(solution)/shard_map/ppermute | solution.py:356
  315.0 13.2 %collective-permute-start.18 = (bf16[384,768]{1,0:T(8,128)(2,1)S(1)}, bf16[384,768]{1,0:T(8,128)(2,1)S(1)}, u32[]{:S(2)}, u32[]{:S(2)}) collective-permute-start(bf16[384,768]{1,0:T(8,128)(2,1)S(1)} %dynamic-slice_convert_fusion.4), channel_id=1, source_target_pairs={{0,4},{2,6},{4,0},{6,2},{8,12},{10,14},{12,8},{14,10},{16,20},{18,... | collective-permute-start | bytes 1769480 | tf_op jit(solution)/shard_map/ppermute | solution.py:366
  318.6 10.2 %collective-permute-start.29 = (bf16[24,1792]{1,0:T(8,128)(2,1)S(1)}, bf16[24,1792]{1,0:T(8,128)(2,1)S(1)}, u32[]{:S(2)}, u32[]{:S(2)}) collective-permute-start(bf16[24,1792]{1,0:T(8,128)(2,1)S(1)} %dynamic-slice_convert_fusion.9), channel_id=1, source_target_pairs={{0,16},{2,18},{4,20},{6,22},{8,24},{10,26},{12,28},{14,30},{16,0},... | collective-permute-start | bytes 258056 | tf_op jit(solution)/shard_map/ppermute | solution.py:366
  328.9 11.3 %collective-permute-start.30 = (bf16[24,1792]{1,0:T(8,128)(2,1)S(1)}, bf16[24,1792]{1,0:T(8,128)(2,1)S(1)}, u32[]{:S(2)}, u32[]{:S(2)}) collective-permute-start(bf16[24,1792]{1,0:T(8,128)(2,1)S(1)} %add_convert_fusion.2), channel_id=1, source_target_pairs={{0,16},{2,18},{4,20},{6,22},{8,24},{10,26},{12,28},{14,30},{16,0},... | collective-permute-start | bytes 258056 | tf_op jit(solution)/shard_map/ppermute | solution.py:366
  336.5 10.3 %collective-permute-start.20 = (bf16[96,768]{1,0:T(8,128)(2,1)S(1)}, bf16[96,768]{1,0:T(8,128)(2,1)S(1)}, u32[]{:S(2)}, u32[]{:S(2)}) collective-permute-start(bf16[96,768]{1,0:T(8,128)(2,1)S(1)} %dynamic-slice_convert_fusion.8), channel_id=1, source_target_pairs={{0,16},{2,18},{4,20},{6,22},{8,24},{10,26},{12,28},{14,30},{16,0},... | collective-permute-start | bytes 442376 | tf_op jit(solution)/shard_map/ppermute | solution.py:366
  356.4 11.0 %collective-permute-start.32 = (bf16[96,1792]{1,0:T(8,128)(2,1)S(1)}, bf16[96,1792]{1,0:T(8,128)(2,1)S(1)}, u32[]{:S(2)}, u32[]{:S(2)}) collective-permute-start(bf16[96,1792]{1,0:T(8,128)(2,1)S(1)} %pad_maximum_fusion.14), channel_id=1, source_target_pairs={{0,4},{2,6},{4,0},{6,2},{8,12},{10,14},{12,8},{14,10},{16,20},{18,... | collective-permute-start | bytes 1032200 | tf_op jit(solution)/shard_map/ppermute | solution.py:366
  361.4 13.7 %collective-permute-start.23 = (bf16[384,768]{1,0:T(8,128)(2,1)S(1)}, bf16[384,768]{1,0:T(8,128)(2,1)S(1)}, u32[]{:S(2)}, u32[]{:S(2)}) collective-permute-start(bf16[384,768]{1,0:T(8,128)(2,1)S(1)} %pad_maximum_fusion.13), channel_id=1, source_target_pairs={{0,4},{2,6},{4,0},{6,2},{8,12},{10,14},{12,8},{14,10},{16,20},{18,... | collective-permute-start | bytes 1769480 | tf_op jit(solution)/shard_map/ppermute | solution.py:366
  368.4 18.9 %collective-permute-start.33 = (bf16[192,1792]{1,0:T(8,128)(2,1)}, bf16[192,1792]{1,0:T(8,128)(2,1)}, u32[]{:S(2)}, u32[]{:S(2)}) collective-permute-start(bf16[192,1792]{1,0:T(8,128)(2,1)} %pad_maximum_fusion.11), channel_id=1, source_target_pairs={{0,2},{2,0},{4,6},{6,4},{8,10},{10,8},{12,14},{14,12},{16,18},{18,... | collective-permute-start | bytes 2064392 | tf_op jit(solution)/shard_map/ppermute | solution.py:366
  376.3 12.5 %collective-permute-start.24 = (bf16[768,768]{1,0:T(8,128)(2,1)}, bf16[768,768]{1,0:T(8,128)(2,1)}, u32[]{:S(2)}, u32[]{:S(2)}) collective-permute-start(bf16[768,768]{1,0:T(8,128)(2,1)} %pad_maximum_fusion.10), channel_id=1, source_target_pairs={{0,2},{2,0},{4,6},{6,4},{8,10},{10,8},{12,14},{14,12},{16,18},{18,... | collective-permute-start | bytes 3538952 | tf_op jit(solution)/shard_map/ppermute | solution.py:366
  (48 other events, 572.0 us)

commit v3 on v2

--- a/solution.py
+++ b/solution.py
@@ -1,3 +1,5 @@
+import functools
+
 import jax
 import jax.numpy as jnp
 from jax import lax
@@ -90,9 +92,8 @@
 
 
 def forward_kernel(
-    in_ref, cot_ref, pre_ref, w_in_ref, w_dt_ref, cw_ref, cb_ref, bias_ref, log_ref, skip_ref,
-    gain_ref, w_out_ref, heads2_ref,
-    hid_o, xbc_o, dt_o, norm_o, dgate_o, dy_o, r1_o, start_o, gain_o, skip_o,
+    in_ref, pre_ref, w_xbc_ref, w_dt_ref, cw_ref, cb_ref, bias_ref, log_ref, heads2_ref,
+    hid_o, xbc_o, dt_o, x_o, y_o, start_o,
     ext, state, inner,
 ):
     first = pl.program_id(0) == 0
@@ -101,14 +102,12 @@
     def _():
         ext[0:8, :] = jnp.zeros((8, CH), f32)
         state[...] = jnp.zeros_like(state)
-        gain_o[...] = jnp.zeros_like(gain_o)
-        skip_o[...] = jnp.zeros_like(skip_o)
 
     values = in_ref[...].astype(f32)
     scale = lax.rsqrt(jnp.mean(values * values, axis=-1, keepdims=True) + EPS)
     hidden = (values * scale * pre_ref[...]).astype(bf16)
     hid_o[...] = hidden
-    xbc = nn(hidden, w_in_ref[:, E:])
+    xbc = nn(hidden, w_xbc_ref[...])
     xbc_o[...] = xbc
     ext[8:, :] = xbc
     dt = nn(hidden, w_dt_ref[...])
@@ -142,13 +141,27 @@
         inner[:, lanes] = total
     start = state[...].astype(bf16)
     start_o[0] = start
-    y_inner = inner[...] + nn(c, start) * spread_heads(jnp.exp(cum), heads2)
+    y_o[...] = inner[...] + nn(c, start) * spread_heads(jnp.exp(cum), heads2)
+    x_o[...] = x
     to_last = (xd.astype(f32) * spread_heads(jnp.exp(last - cum), heads2)).astype(bf16)
     whole = spread_heads(jnp.broadcast_to(jnp.exp(last), (8, PAD)), heads2)[0:1, :]
     state[...] = whole * state[...] + tn(b, to_last)
 
+
+def gate_kernel(
+    hid_ref, x_ref, y_ref, cot_ref, w_gate_ref, skip_ref, gain_ref, w_out_ref, heads2_ref,
+    norm_o, dgate_o, dy_o, r1_o, gain_o, skip_o,
+):
+    @pl.when(pl.program_id(0) == 0)
+    def _():
+        gain_o[...] = jnp.zeros_like(gain_o)
+        skip_o[...] = jnp.zeros_like(skip_o)
+
+    x = x_ref[...]
+    y_inner = y_ref[...]
+    heads2 = heads2_ref[...]
     y = y_inner + skip_ref[...] * x
-    gate = nn(hidden, w_in_ref[:, :E])
+    gate = nn(hid_ref[...], w_gate_ref[...])
     sig = sigmoid(gate)
     opened = gate * sig
     gated = y * opened
@@ -169,25 +182,24 @@
 
 
 def backward_kernel(
-    xbc_ref, before_ref, dt_ref, dy_ref, r1_ref, start_ref, cw_ref, cb_ref, bias_ref, log_ref,
-    skip_ref, heads2_ref,
-    dxbc_o, ddt_o, gcw_o, gcb_o, gbias_o, glog_o,
+    end, xbc_ref, before_ref, dt_ref, dy_ref, r1_ref, start_ref, cw_ref, cb_ref, bias_ref, log_ref,
+    skip_ref, heads2_ref, state_ref, head_ref,
+    dxbc_o, ddt_o, gcw_o, gcb_o, gbias_o, glog_o, state_o, head_o,
     ext, ext_back, d_state, d_inner, d_scores,
 ):
     step_id = pl.program_id(0)
-    steps = pl.num_programs(0)
 
     @pl.when(step_id == 0)
     def _():
-        ext_back[BLOCK:, :] = jnp.zeros((8, CH), f32)
-        d_state[...] = jnp.zeros_like(d_state)
+        ext_back[BLOCK:, :] = head_ref[...]
+        d_state[...] = state_ref[...]
         gcw_o[...] = jnp.zeros_like(gcw_o)
         gcb_o[...] = jnp.zeros_like(gcb_o)
         gbias_o[...] = jnp.zeros_like(gbias_o)
         glog_o[...] = jnp.zeros_like(glog_o)
 
     xbc = xbc_ref[...]
-    ext[0:8, :] = jnp.where(step_id == steps - 1, 0.0, before_ref[...])
+    ext[0:8, :] = jnp.where(step_id == end - 1, 0.0, before_ref[...])
     ext[8:, :] = xbc
     cw = cw_ref[...]
     summed = conv_sum(ext, cw, cb_ref[...])
@@ -265,31 +277,31 @@
     dxbc_o[...] = total.astype(bf16)
     head = ext_back[0:8, :]
     ext_back[BLOCK:, :] = head
+    head_o[...] = head
+    state_o[...] = d_state[...]
 
 
 def whole_spec(shape):
     return pl.BlockSpec(shape, lambda i: tuple(0 for _ in shape))
 
 
-def forward_call(seq, cot, pre, w_in, w_dt, cw, cb, bias, log_rate, skip, gain, w_out, heads2):
+def forward_call(seq, pre, w_xbc, w_dt, cw, cb, bias, log_rate, heads2):
     tokens, width = seq.shape
     blocks = tokens // BLOCK
     rows = lambda n: pl.BlockSpec((BLOCK, n), lambda i: (i, 0))
     out = jax.ShapeDtypeStruct
-    weights = (pre, w_in, w_dt, cw, cb, bias, log_rate, skip, gain, w_out, heads2)
+    weights = (pre, w_xbc, w_dt, cw, cb, bias, log_rate, heads2)
     return pl.pallas_call(
         forward_kernel,
         grid=(blocks,),
-        in_specs=[rows(width), rows(width)] + [whole_spec(w.shape) for w in weights],
+        in_specs=[rows(width)] + [whole_spec(w.shape) for w in weights],
         out_specs=[
-            rows(width), rows(CH), rows(PAD), rows(E), rows(E), rows(E), rows(PAD),
+            rows(width), rows(CH), rows(PAD), rows(E), rows(E),
             pl.BlockSpec((1, N, E), lambda i: (i, 0, 0)),
-            whole_spec((1, E)), whole_spec((1, E)),
         ],
         out_shape=[
             out((tokens, width), bf16), out((tokens, CH), f32), out((tokens, PAD), f32),
-            out((tokens, E), bf16), out((tokens, E), bf16), out((tokens, E), bf16),
-            out((tokens, PAD), f32), out((blocks, N, E), bf16), out((1, E), f32), out((1, E), f32),
+            out((tokens, E), f32), out((tokens, E), f32), out((blocks, N, E), bf16),
         ],
         scratch_shapes=[
             pltpu.VMEM((BLOCK + 8, CH), f32), pltpu.VMEM((N, E), f32), pltpu.VMEM((BLOCK, E), f32),
@@ -299,33 +311,59 @@
             flops=20_000_000_000, bytes_accessed=40_000_000, transcendentals=12_000_000
         ),
         name="mixer_forward",
-    )(seq, cot, *weights)
-
-
-def backward_call(xbc, dt, dy, r1, starts, cw, cb, bias, log_rate, skip, heads2):
-    tokens = xbc.shape[0]
-    blocks = tokens // BLOCK
+    )(seq, *weights)
+
+
+def gate_call(hidden, x, y, cot, w_gate, skip, gain, w_out, heads2):
+    tokens, width = hidden.shape
+    rows = lambda n: pl.BlockSpec((BLOCK, n), lambda i: (i, 0))
+    out = jax.ShapeDtypeStruct
+    weights = (w_gate, skip, gain, w_out, heads2)
+    return pl.pallas_call(
+        gate_kernel,
+        grid=(tokens // BLOCK,),
+        in_specs=[rows(width), rows(E), rows(E), rows(width)]
+        + [whole_spec(w.shape) for w in weights],
+        out_specs=[
+            rows(E), rows(E), rows(E), rows(PAD), whole_spec((1, E)), whole_spec((1, E)),
+        ],
+        out_shape=[
+            out((tokens, E), bf16), out((tokens, E), bf16), out((tokens, E), bf16),
+            out((tokens, PAD), f32), out((1, E), f32), out((1, E), f32),
+        ],
+        compiler_params=pltpu.CompilerParams(vmem_limit_bytes=VMEM),
+        cost_estimate=pl.CostEstimate(
+            flops=6_000_000_000, bytes_accessed=30_000_000, transcendentals=3_000_000
+        ),
+        name="gated_norm",
+    )(hidden, x, y, cot, *weights)
+
+
+def backward_call(begin, end, xbc, dt, dy, r1, starts, weights, d_state, head):
     per = BLOCK // 8
-    rows = lambda n: pl.BlockSpec((BLOCK, n), lambda i: (blocks - 1 - i, 0))
+    tokens = (end - begin) * BLOCK
+    rows = lambda n: pl.BlockSpec((BLOCK, n), lambda i: (end - 1 - i, 0))
+    outs = lambda n: pl.BlockSpec((BLOCK, n), lambda i: (end - begin - 1 - i, 0))
     out = jax.ShapeDtypeStruct
-    weights = (cw, cb, bias, log_rate, skip, heads2)
+    weights = (*weights, d_state, head)
     return pl.pallas_call(
-        backward_kernel,
-        grid=(blocks,),
+        functools.partial(backward_kernel, end),
+        grid=(end - begin,),
         in_specs=[
             rows(CH),
-            pl.BlockSpec((8, CH), lambda i: (jnp.maximum((blocks - 1 - i) * per - 1, 0), 0)),
+            pl.BlockSpec((8, CH), lambda i: (jnp.maximum((end - 1 - i) * per - 1, 0), 0)),
             rows(PAD), rows(E), rows(PAD),
-            pl.BlockSpec((1, N, E), lambda i: (blocks - 1 - i, 0, 0)),
+            pl.BlockSpec((1, N, E), lambda i: (end - 1 - i, 0, 0)),
         ]
         + [whole_spec(w.shape) for w in weights],
         out_specs=[
-            rows(CH), rows(PAD), whole_spec((K, CH)), whole_spec((1, CH)), whole_spec((1, PAD)),
-            whole_spec((1, PAD)),
+            outs(CH), outs(PAD), whole_spec((K, CH)), whole_spec((1, CH)), whole_spec((1, PAD)),
+            whole_spec((1, PAD)), whole_spec((N, E)), whole_spec((8, CH)),
         ],
         out_shape=[
             out((tokens, CH), bf16), out((tokens, PAD), bf16), out((K, CH), f32),
-            out((1, CH), f32), out((1, PAD), f32), out((1, PAD), f32),
+            out((1, CH), f32), out((1, PAD), f32), out((1, PAD), f32), out((N, E), f32),
+            out((8, CH), f32),
         ],
         scratch_shapes=[
             pltpu.VMEM((BLOCK + 8, CH), f32), pltpu.VMEM((BLOCK + 8, CH), f32),
@@ -333,7 +371,7 @@
         ],
         compiler_params=pltpu.CompilerParams(vmem_limit_bytes=VMEM),
         cost_estimate=pl.CostEstimate(
-            flops=20_000_000_000, bytes_accessed=30_000_000, transcendentals=12_000_000
+            flops=20_000_000_000, bytes_accessed=20_000_000, transcendentals=6_000_000
         ),
         name="mixer_backward",
     )(xbc, xbc, dt, dy, r1, starts, *weights)
@@ -387,21 +425,48 @@
     return in_order(shard, part.reshape(rows, columns), mine)
 
 
-def summed_over_all(halves, mine):
+def halved(halves, mine):
     kept = lax.dynamic_index_in_dim(halves, mine, 0, keepdims=False)
-    sent = lax.dynamic_index_in_dim(halves, 1 - mine, 0, keepdims=False).astype(SEND)
-    total = kept + lax.ppermute(sent, "grp", SWAP).astype(f32)
+    sent = lax.dynamic_index_in_dim(halves, 1 - mine, 0, keepdims=False)
+    return kept, sent.astype(SEND)
+
+
+def core_halves(v):
+    half = v.shape[1] // 2
+    high = bit_of(0)
+    kept = lax.dynamic_slice_in_dim(v, high * half, half, axis=1)
+    sent = lax.dynamic_slice_in_dim(v, (1 - high) * half, half, axis=1)
+    return kept, sent.astype(SEND)
+
+
+def shifted(v, bit, count, mask):
+    size = lax.axis_size("rep")
+    return lax.ppermute(v, "rep", [(i, i ^ (mask << bit)) for i in range(size)])
+
+
+def summed_over_rest(total):
     bits = (lax.axis_size("rep") - 1).bit_length()
-    for bit in range(bits):
-        half = total.shape[0] // 2
-        high = bit_of(bit)
-        kept = lax.dynamic_slice_in_dim(total, high * half, half, axis=0)
-        sent = lax.dynamic_slice_in_dim(total, (1 - high) * half, half, axis=0).astype(SEND)
-        total = kept + flipped(sent, bit).astype(f32)
+    groups = [(1, 1)] + [(b, min(2, bits - b)) for b in range(2, bits, 2)]
+    for bit, width in groups:
+        count = 1 << width
+        me = (lax.axis_index("rep") >> bit) & (count - 1)
+        size = total.shape[0] // count
+        part = lambda mask: lax.dynamic_slice_in_dim(total, (me ^ mask) * size, size, axis=0)
+        come = [shifted(part(m).astype(SEND), bit, count, m) for m in range(1, count)]
+        total = sum((v.astype(f32) for v in come), part(0))
     total = total.astype(SEND)
-    for bit in reversed(range(bits)):
-        total = in_order(total, flipped(total, bit), bit_of(bit))
-    return total.astype(f32)
+    for bit, width in reversed(groups):
+        count = 1 << width
+        me = (lax.axis_index("rep") >> bit) & (count - 1)
+        parts = [total] + [shifted(total, bit, count, m) for m in range(1, count)]
+        ordered = []
+        for place in range(count):
+            pick = parts[0]
+            for m in range(1, count):
+                pick = jnp.where((me ^ m) == place, parts[m], pick)
+            ordered.append(pick)
+        total = jnp.concatenate(ordered, axis=0)
+    return total
 
 
 def summed_small(halves, mine):
@@ -433,29 +498,59 @@
     wdt = pad_heads(both[:, at:].reshape(-1, H))
     bias, log_rate = pad_heads(bias), pad_heads(log_rate)
     skip = jnp.repeat(skip, P_SIZE, axis=1)
-    win = gathered_rows(w_in, mine)
+    seq = to_sequence(inputs, mine)
+    w_xbc = gathered_rows(w_in[:, E:], mine)
+    w_gate, w_out, cotangent, _, _ = lax.optimization_barrier(
+        (w_in[:, :E], w_out, cotangent, seq, w_xbc)
+    )
+    w_gate = gathered_rows(w_gate, mine)
+    cot = to_sequence(cotangent, mine)
     wout = gathered_rows(w_out, mine)
     heads = (jnp.arange(PAD)[:, None] == jnp.arange(E)[None, :] // P_SIZE).astype(bf16)
     heads2 = jnp.concatenate([heads, heads], axis=0)
-    seq = to_sequence(inputs, mine)
-    cot = to_sequence(cotangent, mine)
-    hidden, xbc, dt, normed, d_gate, dy, r1, starts, g_gain, g_skip = forward_call(
-        seq, cot, pre, win, wdt, cw, cb, bias, log_rate, skip, gain, wout, heads2
+    hidden, xbc, dt, x, y, starts = forward_call(
+        seq, pre, w_xbc, wdt, cw, cb, bias, log_rate, heads2
+    )
+    normed, d_gate, dy, r1, g_gain, g_skip = gate_call(
+        hidden, x, y, cot, w_gate, skip, gain, wout, heads2
     )
     g_out = tn(normed, cot).reshape(2, E // 2, -1)
     g_gate = tn(hidden, d_gate).reshape(2, -1, E)
     early = jnp.concatenate([g_out, g_gate[:, :, : E // 2], g_gate[:, :, E // 2 :]], axis=1)
-    early = summed_over_all(early, mine)
+    early_kept, early_sent = halved(early, mine)
+    early_sent, dy = lax.optimization_barrier((early_sent, dy))
+    early_come = lax.ppermute(early_sent, "grp", SWAP)
     third = w_in.shape[0]
+    result = to_pieces((seq.astype(f32) + nn(normed, wout)).astype(bf16), mine)
+    weights = (cw, cb, bias, log_rate, skip, heads2)
+    blocks = xbc.shape[0] // BLOCK
+    middle = blocks // 2
+    high = backward_call(
+        middle, blocks, xbc, dt, dy, r1, starts, weights, jnp.zeros((N, E), f32),
+        jnp.zeros((8, CH), f32),
+    )
+    d_state, head, early_come = lax.optimization_barrier((high[6], high[7], early_come))
+    early = early_kept + early_come.astype(f32)
+    early_kept, early_sent = core_halves(early[None])
+    early_sent, d_state = lax.optimization_barrier((early_sent, d_state))
+    early_other = flipped(early_sent, 0)
+    low = backward_call(0, middle, xbc, dt, dy, r1, starts, weights, d_state, head)
+    d_xbc, d_dt = (jnp.concatenate([low[i], high[i]], axis=0) for i in range(2))
+    g_cw, g_cb, g_bias, g_log = (low[i] + high[i] for i in range(2, 6))
+    late = tn(hidden, d_xbc).reshape(2, -1, CH)
+    late_kept, late_sent = core_halves(late)
+    late = late_kept + flipped(late_sent, 0).astype(f32)
+    late_kept, late_sent = halved(late, mine)
+    late = late_kept + lax.ppermute(late_sent, "grp", SWAP).astype(f32)
+    late = summed_over_rest(late)
+    grad_xbc_w = in_order(late, flipped(late, 0), bit_of(0)).astype(f32)
+    early = (early_kept + early_other.astype(f32))[0]
+    early = summed_over_rest(early)
+    early = in_order(early, flipped(early, 0), bit_of(0)).astype(f32)
     grad_out_w = early[: E // 2]
     grad_gate_w = jnp.concatenate([early[E // 2 : E // 2 + third], early[E // 2 + third :]], axis=1)
-    result = to_pieces((seq.astype(f32) + nn(normed, wout)).astype(bf16), mine)
-    d_xbc, d_dt, g_cw, g_cb, g_bias, g_log = backward_call(
-        xbc, dt, dy, r1, starts, cw, cb, bias, log_rate, skip, heads2
-    )
-    grad_xbc_w = summed_over_all(tn(hidden, d_xbc).reshape(2, -1, CH), mine)
     grad_in_w = jnp.concatenate([grad_gate_w, grad_xbc_w], axis=1)
-    d_hidden = nt(d_gate, win[:, :E]) + nt(d_xbc, win[:, E:]) + nt(d_dt, wdt)
+    d_hidden = nt(d_gate, w_gate) + nt(d_xbc, w_xbc) + nt(d_dt, wdt)
     seq32 = seq.astype(f32)
     scale = lax.rsqrt(jnp.mean(seq32 * seq32, axis=-1, keepdims=True) + EPS)
     unit = seq32 * scale

time: 401 us -> 397 us (0.990)
  waiting for transfers between devices: 132 us -> 111 us
  local copies, waits for them, and re-layouts: 45.3 us -> 59 us
  Pallas kernels: 87 us -> 96.3 us
    ppermute x2, waiting for transfers between devices: 30.7 us -> 0.01 us  [to_sequence(): lax.ppermute(lax.dynamic_index_in_dim(pieces, 1 - mine, 0, keepdims=False...]
    ppermute x24 -> x14, waiting for transfers between devices: 43.9 us -> 18.3 us  [flipped(): return lax.ppermute(v, 'rep', [(i, i ^ 1 << bit) for i in range(size)])]
    ppermute x24 -> x14, starting transfers between devices: 31.3 us -> 9.3 us  [flipped(): return lax.ppermute(v, 'rep', [(i, i ^ 1 << bit) for i in range(size)])]
    ppermute x2 -> x18, waiting for transfers between devices: 50.6 us -> 68.8 us  [the longest x16 43 us: shifted(): return lax.ppermute(v, 'rep', [(i, i ^ mask << bit) for i in range(size)])]
    ppermute x2 -> x18, starting transfers between devices: 2.09 us -> 18.6 us  [the longest x16 16.9 us: shifted(): return lax.ppermute(v, 'rep', [(i, i ^ mask << bit) for i in range(size)])]
    pallas_call x2 -> x4, Pallas kernels: 87 us -> 96.3 us  [the longest x2 52.3 us: backward_call(): pl.pallas_call(functools.partial(backward_kernel, end), grid=(end - begin...]
    ppermute x1, waiting for transfers between devices: 0.01 us -> 9.11 us  [per_device(): lax.ppermute(vectors[None], 'grp', SWAP)]
    add x8 -> x10, other arithmetic: 3.52 us -> 11.5 us  [the longest x1 3.51 us: per_device(): early = early_kept + early_come.astype(f32)]
  transfers between devices with their start and end apart: 34 -> 41, of which waited for: 17 -> 18; matrix products, arithmetic and copies ran while one was open for 18% -> 28% of each run, Pallas kernels for 0% -> 20%
where the time goes in v3:
time: 397 us; the launch traced here: 393 us
  waiting for transfers between devices  111 us (28%)
  Pallas kernels  96.3 us (24%)
  local copies, waits for them, and re-layouts  59 us (15%)
  other arithmetic  50 us (13%)
  starting transfers between devices  40.2 us (10%)
  matrix products  34 us (9%)
    pallas_call x2, Pallas kernels, backward_call(): pl.pallas_call(functools.partial(backward_kernel, end), grid=(end - begin...  52.3 us
    ppermute x16, waiting for transfers between devices, shifted(): return lax.ppermute(v, 'rep', [(i, i ^ mask << bit) for i in range(size)])  43 us
    pallas_call x1, Pallas kernels, forward_call(): pl.pallas_call(forward_kernel, grid=(blocks,), in_specs=[rows(width)] + [...  25 us
    pallas_call x1, Pallas kernels, gate_call(): pl.pallas_call(gate_kernel, grid=(tokens // BLOCK,), in_specs=[rows(width...  19 us
    ppermute x14, waiting for transfers between devices, flipped(): return lax.ppermute(v, 'rep', [(i, i ^ 1 << bit) for i in range(size)])  18.3 us
    dot_general x3, matrix products, nt(): lax.dot_general(a, b, (((1,), (1,)), ((), ())), preferred_element_type=f32)  18 us
    ppermute x16, starting transfers between devices, shifted(): return lax.ppermute(v, 'rep', [(i, i ^ mask << bit) for i in range(size)])  16.9 us
    ppermute x1, waiting for transfers between devices, per_device(): early_come = lax.ppermute(early_sent, 'grp', SWAP)  16.9 us
  transfers between devices with their start and end apart: 41, of which 18 were waited for; matrix products, arithmetic and copies ran while one was open for 28% of the time, Pallas kernels for 20%

profile of v3, /device:TPU:0, one launch (start us, length us, event | category | flops | bytes accessed | tf_op | source)
XLA Modules:
  0.0 392.7 jit_solution(5061889522818000155)
XLA Ops:
  6.7 4.2 %concatenate.78 = bf16[14884]{0:T(1024)(128)(2,1)S(1)} concatenate(bf16[3584]{0:T(1024)(128)(2,1)S(1)} %reshape.240, bf16[384]{0:T(512)(128)(2,1)} %param.13, bf16[896]{0:T(1024)(128)(2,1)} %param.17, bf16[12]{0:T(256)(128)(2,1)} %param.18, bf16[12]{0:T(256)(128)(2,1)} %param.19, bf16[12]{0:T(256)(128)(2,1)} %param.20, bf16[768]{0:T(1024)(128)(2,1)} %param.21, ...), dimensions={0} | concatenate | bytes 59536 | tf_op jit(solution)/shard_map/concatenate | solution.py:486
  15.5 9.1 %collective-permute-done.1 = bf16[1,14884]{1,0:T(2,128)(2,1)S(1)} collective-permute-done((bf16[1,14884]{1,0:T(2,128)(2,1)S(1)}, bf16[1,14884]{1,0:T(2,128)(2,1)S(1)}, u32[]{:S(2)}, u32[]{:S(2)}) %collective-permute-start.1) | collective-permute-done | bytes 29800 | tf_op jit(solution)/shard_map/ppermute | solution.py:489
  25.0 6.1 %collective-permute-done.2 = bf16[96,1792]{1,0:T(8,128)(2,1)S(1)} collective-permute-done((bf16[96,1792]{1,0:T(8,128)(2,1)S(1)}, bf16[96,1792]{1,0:T(8,128)(2,1)S(1)}, u32[]{:S(2)}, u32[]{:S(2)}) %collective-permute-start.2) | collective-permute-done | bytes 344096 | tf_op jit(solution)/shard_map/ppermute | solution.py:422
  33.0 7.4 %collective-permute-done.3 = bf16[1,1,96,1792]{3,2,1,0:T(8,128)(2,1)S(1)} collective-permute-done((bf16[1,1,96,1792]{3,2,1,0:T(8,128)(2,1)S(1)}, bf16[1,1,96,1792]{3,2,1,0:T(8,128)(2,1)S(1)}, u32[]{:S(2)}, u32[]{:S(2)}) %collective-permute-start.3) | collective-permute-done | bytes 344096 | tf_op jit(solution)/shard_map/ppermute | solution.py:404
  58.9 5.2 %collective-permute-done.6 = bf16[96,1536]{1,0:T(8,128)(2,1)S(1)} collective-permute-done((bf16[96,1536]{1,0:T(8,128)(2,1)S(1)}, bf16[96,1536]{1,0:T(8,128)(2,1)S(1)}, u32[]{:S(2)}, u32[]{:S(2)}) %collective-permute-start.6) | collective-permute-done | bytes 294944 | tf_op jit(solution)/shard_map/ppermute | solution.py:422
  65.6 25.0 %mixer_forward.1 = (bf16[1024,768]{1,0:T(8,128)(2,1)}, f32[1024,1792]{1,0:T(8,128)}, f32[1024,128]{1,0:T(8,128)}, f32[1024,1536]{1,0:T(8,128)}, f32[1024,1536]{1,0:T(8,128)}, /*index=5*/bf16[4,128,1536]{2,1,0:T(8,128)(2,1)}) custom-call(bf16[1024,768]{1,0:T(8,128)(2,1)} %pad_maximum_fusion.5.in_ref, f32[1,768]{1,0:T(1,128)} %bitcast.106, ...), custom_call_target="tpu_custom_call" | custom-call | flops 20000000000 | bytes 40000000 | tf_op jit(solution)/shard_map/mixer_forward/pallas_call | solution.py:294
  91.4 7.2 %collective-permute-done.10 = bf16[1,1,192,768]{3,2,1,0:T(8,128)(2,1)S(1)} collective-permute-done((bf16[1,1,192,768]{3,2,1,0:T(8,128)(2,1)S(1)}, bf16[1,1,192,768]{3,2,1,0:T(8,128)(2,1)S(1)}, u32[]{:S(2)}, u32[]{:S(2)}) %collective-permute-start.10) | collective-permute-done | bytes 294944 | tf_op jit(solution)/shard_map/ppermute | solution.py:404
  106.3 19.0 %gated_norm.1 = (bf16[1024,1536]{1,0:T(8,128)(2,1)}, bf16[1024,1536]{1,0:T(8,128)(2,1)}, bf16[1024,1536]{1,0:T(8,128)(2,1)}, f32[1024,128]{1,0:T(8,128)}, f32[1,1536]{1,0:T(1,128)}, /*index=5*/f32[1,1536]{1,0:T(1,128)}) custom-call(bf16[1024,768]{1,0:T(8,128)(2,1)} %get-tuple-element.48.hid_ref, f32[1024,1536]{1,0:T(8,128)} %get-tuple-element.49.x_ref, ...), custom_call_target="tpu_custom_call" | custom-call | flops 6000000000 | bytes 30000000 | tf_op jit(solution)/shard_map/gated_norm/pallas_call | solution.py:322
  125.4 4.6 %fusion.9 = bf16[1024,768]{1,0:T(8,128)(2,1)S(1)} fusion(bf16[1024,1536]{1,0:T(8,128)(2,1)} %get-tuple-element.54, bf16[768,768]{1,0:T(8,128)(2,1)S(1)} %get-tuple-element.109, bf16[768,768]{1,0:T(8,128)(2,1)S(1)} %get-tuple-element.108, bf16[512,768]{1,0:T(8,128)(2,1)S(1)} %get-tuple-element.115, bf16[512,768]{1,0:T(8,128)(2,1)S(1)} %get-tuple-element.114), kind=kOutput, calls=%fused_computation.16 | convolution fusion | flops 2425356288 | bytes 8650752 | tf_op jit(solution)/shard_map/dot_general | solution.py:28
  130.1 4.3 %fusion.24 = f32[1536,768]{1,0:T(8,128)} fusion(bf16[1024,1536]{1,0:T(8,128)(2,1)S(1)} %copy-done.30, bf16[512,768]{1,0:T(8,128)(2,1)S(1)} %get-tuple-element.113, bf16[512,768]{1,0:T(8,128)(2,1)S(1)} %get-tuple-element.112), kind=kOutput, calls=%fused_computation.149 | convolution fusion | flops 2419064832 | bytes 9437184 | tf_op jit(solution)/shard_map/dot_general | solution.py:36
  142.4 8.0 %pad_maximum_fusion = f32[2,1536,768]{2,1,0:T(8,128)} fusion(f32[2,384,768]{2,1,0:T(8,128)} %get-tuple-element.101, f32[2,384,768]{2,1,0:T(8,128)} %get-tuple-element.100, f32[2,768,768]{2,1,0:T(8,128)} %bitcast.92), kind=kLoop, calls=%fused_computation | loop fusion | flops 4718592 | bytes 18874368 | tf_op jit(solution)/shard_map/concatenate | solution.py:519
  150.5 4.0 %fusion.11 = bf16[1536,768]{1,0:T(8,128)(2,1)} fusion(f32[2,1536,768]{2,1,0:T(8,128)} %pad_maximum_fusion, s32[]{:T(128)S(6)} %select_n.442), kind=kLoop, calls=%fused_computation.22 | loop fusion | bytes 4718596 | tf_op jit(solution)/shard_map/convert_element_type | solution.py:431
  156.7 6.8 %fusion.22 = f32[1024,768]{1,0:T(8,128)} fusion(bf16[1024,1536]{1,0:T(8,128)(2,1)} %get-tuple-element.55, bf16[384,1536]{1,0:T(8,128)(2,1)} %copy-done.15, bf16[384,1536]{1,0:T(8,128)(2,1)} %copy-done.14), kind=kOutput, calls=%fused_computation.147 | convolution fusion | flops 2420637696 | bytes 8650752 | tf_op jit(solution)/shard_map/dot_general | solution.py:32
  165.1 26.2 %mixer_backward.2 = (bf16[512,1792]{1,0:T(8,128)(2,1)}, bf16[512,128]{1,0:T(8,128)(2,1)}, f32[4,1792]{1,0:T(4,128)}, f32[1,1792]{1,0:T(1,128)}, f32[1,128]{1,0:T...) custom-call(f32[1024,1792]{1,0:T(8,128)} %get-tuple-element.56.xbc_ref.before_ref, ...), custom_call_target="tpu_custom_call" | custom-call | flops 20000000000 | bytes 20000000 | tf_op jit(solution)/shard_map/mixer_backward/pallas_call | solution.py:349
  191.3 16.9 %collective-permute-done.13 = bf16[1536,768]{1,0:T(8,128)(2,1)} collective-permute-done((bf16[1536,768]{1,0:T(8,128)(2,1)}, bf16[1536,768]{1,0:T(8,128)(2,1)}, u32[]{:S(2)}, u32[]{:S(2)}) %collective-permute-start.13) | collective-permute-done | bytes 2359328 | tf_op jit(solution)/shard_map/ppermute | solution.py:522
  215.1 26.1 %mixer_backward.3 = (bf16[512,1792]{1,0:T(8,128)(2,1)}, bf16[512,128]{1,0:T(8,128)(2,1)}, f32[4,1792]{1,0:T(4,128)}, f32[1,1792]{1,0:T(1,128)}, f32[1,128]{1,0:T...) custom-call(f32[1024,1792]{1,0:T(8,128)} %get-tuple-element.56.xbc_ref.before_ref, ...), custom_call_target="tpu_custom_call" | custom-call | flops 20000000000 | bytes 20000000 | tf_op jit(solution)/shard_map/mixer_backward/pallas_call | solution.py:349
  244.8 4.8 %fusion.23 = f32[1024,768]{1,0:T(8,128)} fusion(bf16[1024,1792]{1,0:T(8,128)(2,1)S(1)} %constant_dynamic-update-slice_fusion, bf16[384,1792]{1,0:T(8,128)(2,1)S(1)} %copy-done.13, bf16[384,1792]{1,0:T(8,128)(2,1)S(1)} %copy-done.11), kind=kOutput, calls=%fused_computation.148 | convolution fusion | flops 2824077312 | bytes 9568256 | tf_op jit(solution)/shard_map/dot_general | solution.py:32
  260.3 6.4 %fusion.8 = (f32[768]{0:T(1024)S(1)}, f32[1024]{0:T(1024)}, f32[1024,768]{1,0:T(8,128)}) fusion(f32[1024]{0:T(1024)S(1)} %add_rsqrt_fusion, bf16[512,768]{1,0:T(8,128)(2,1)S(1)} %get-tuple-element.115, bf16[512,768]{1,0:T(8,128)(2,1)S(1)} %get-tuple-element.114, f32[768]{0:T(1024)S(1)} %reshape.266, bf16[1024,128]{1,0:T(8,128)(2,1)} %copy-done.22, ...), kind=kOutput, calls=%fused_computation.15 | convolution fusion | flops 210761984 | bytes 11323392 | tf_op jit(solution)/shard_map/dot_general | solution.py:32
  304.6 9.0 %collective-permute-done.31 = bf16[192,1792]{1,0:T(8,128)(2,1)S(1)} collective-permute-done((bf16[192,1792]{1,0:T(8,128)(2,1)S(1)}, bf16[192,1792]{1,0:T(8,128)(2,1)S(1)}, u32[]{:S(2)}, u32[]{:S(2)}) %collective-permute-start.31) | collective-permute-done | bytes 688160 | tf_op jit(solution)/shard_map/ppermute | solution.py:544
  335.1 8.0 %collective-permute-done.34 = bf16[24,1792]{1,0:T(8,128)(2,1)S(1)} collective-permute-done((bf16[24,1792]{1,0:T(8,128)(2,1)S(1)}, bf16[24,1792]{1,0:T(8,128)(2,1)S(1)}, u32[]{:S(2)}, u32[]{:S(2)}) %collective-permute-start.34) | collective-permute-done | bytes 86048 | tf_op jit(solution)/shard_map/ppermute | solution.py:444
  346.8 7.7 %collective-permute-done.23 = bf16[96,768]{1,0:T(8,128)(2,1)S(1)} collective-permute-done((bf16[96,768]{1,0:T(8,128)(2,1)S(1)}, bf16[96,768]{1,0:T(8,128)(2,1)S(1)}, u32[]{:S(2)}, u32[]{:S(2)}) %collective-permute-start.23) | collective-permute-done | bytes 147488 | tf_op jit(solution)/shard_map/ppermute | solution.py:444
  359.2 4.0 %collective-permute-done.38 = bf16[24,1792]{1,0:T(8,128)(2,1)S(1)} collective-permute-done((bf16[24,1792]{1,0:T(8,128)(2,1)S(1)}, bf16[24,1792]{1,0:T(8,128)(2,1)S(1)}, u32[]{:S(2)}, u32[]{:S(2)}) %collective-permute-start.38) | collective-permute-done | bytes 86048 | tf_op jit(solution)/shard_map/ppermute | solution.py:444
  368.2 5.0 %collective-permute-done.39 = bf16[96,1792]{1,0:T(8,128)(2,1)S(1)} collective-permute-done((bf16[96,1792]{1,0:T(8,128)(2,1)S(1)}, bf16[96,1792]{1,0:T(8,128)(2,1)S(1)}, u32[]{:S(2)}, u32[]{:S(2)}) %collective-permute-start.39) | collective-permute-done | bytes 344096 | tf_op jit(solution)/shard_map/ppermute | solution.py:444
  373.4 9.9 %collective-permute-done.28 = bf16[384,768]{1,0:T(8,128)(2,1)S(1)} collective-permute-done((bf16[384,768]{1,0:T(8,128)(2,1)S(1)}, bf16[384,768]{1,0:T(8,128)(2,1)S(1)}, u32[]{:S(2)}, u32[]{:S(2)}) %collective-permute-start.28) | collective-permute-done | bytes 589856 | tf_op jit(solution)/shard_map/ppermute | solution.py:444
  (277 shorter events, 156.0 us)
Async XLA Ops:
  2.0 44.5 %collective-permute-start = (bf16[512,768]{1,0:T(8,128)(2,1)S(1)}, bf16[512,768]{1,0:T(8,128)(2,1)}, u32[]{:S(2)}, u32[]{:S(2)}) collective-permute-start(bf16[512,768]{1,0:T(8,128)(2,1)S(1)} %dynamic-slice_bitcast_fusion.3), channel_id=1, source_target_pairs={{0,1},{1,0},{2,3},{3,2},{4,5},{5,4},{6,7},{7,6},{8,9},{9,8},{10,11... | collective-permute-start | bytes 2359304 | tf_op jit(solution)/shard_map/ppermute | solution.py:385
  10.9 13.7 %collective-permute-start.1 = (bf16[1,14884]{1,0:T(2,128)(2,1)S(1)}, bf16[1,14884]{1,0:T(2,128)(2,1)S(1)}, u32[]{:S(2)}, u32[]{:S(2)}) collective-permute-start(bf16[1,14884]{1,0:T(2,128)(2,1)S(1)} %broadcast_in_dim.29), channel_id=1, source_target_pairs={{0,1},{1,0},{2,3},{3,2},{4,5},{5,4},{6,7},{7,6},{8,9},{9,8},{10,11... | collective-permute-start | bytes 89312 | tf_op jit(solution)/shard_map/ppermute | solution.py:489
  11.0 20.1 %collective-permute-start.2 = (bf16[96,1792]{1,0:T(8,128)(2,1)S(1)}, bf16[96,1792]{1,0:T(8,128)(2,1)S(1)}, u32[]{:S(2)}, u32[]{:S(2)}) collective-permute-start(bf16[96,1792]{1,0:T(8,128)(2,1)S(1)} %constant_dynamic-slice_fusion.4), channel_id=1, source_target_pairs={{0,1},{1,0},{2,3},{3,2},{4,5},{5,4},{6,7},{7,6},{8,9},{9,8},{10,11... | collective-permute-start | bytes 1032200 | tf_op jit(solution)/shard_map/ppermute | solution.py:422
  55.8 43.0 %collective-permute-start.5 = (bf16[512,768]{1,0:T(8,128)(2,1)S(1)}, bf16[512,768]{1,0:T(8,128)(2,1)S(1)}, u32[]{:S(2)}, u32[]{:S(2)}) collective-permute-start(bf16[512,768]{1,0:T(8,128)(2,1)S(1)} %dynamic-slice_bitcast_fusion.2), channel_id=1, source_target_pairs={{0,1},{1,0},{2,3},{3,2},{4,5},{5,4},{6,7},{7,6},{8,9},{9,8},{10,11... | collective-permute-start | bytes 2359304 | tf_op jit(solution)/shard_map/ppermute | solution.py:385
  57.5 33.1 %collective-permute-start.9 = (bf16[192,768]{1,0:T(8,128)(2,1)S(1)}, bf16[192,768]{1,0:T(8,128)(2,1)S(1)}, u32[]{:S(2)}, u32[]{:S(2)}) collective-permute-start(bf16[192,768]{1,0:T(8,128)(2,1)S(1)} %constant_dynamic-slice_fusion.2), channel_id=1, source_target_pairs={{0,1},{1,0},{2,3},{3,2},{4,5},{5,4},{6,7},{7,6},{8,9},{9,8},{10,11... | collective-permute-start | bytes 884744 | tf_op jit(solution)/shard_map/ppermute | solution.py:422
  64.1 27.1 %collective-permute-start.7 = (bf16[1,1,96,1536]{3,2,1,0:T(8,128)(2,1)S(1)}, bf16[1,1,96,1536]{3,2,1,0:T(8,128)(2,1)S(1)}, u32[]{:S(2)}, u32[]{:S(2)}) collective-permute-start(bf16[1,1,96,1536]{3,2,1,0:T(8,128)(2,1)S(1)} %bitcast.96), channel_id=1, source_target_pairs={{0,4},{2,6},{4,0},{6,2},{8,12},{10,14},{12,8},{14,10},{16,20},{18,... | collective-permute-start | bytes 884744 | tf_op jit(solution)/shard_map/ppermute | solution.py:404
  135.7 149.4 %collective-permute-start.12 = (bf16[512,768]{1,0:T(8,128)(2,1)}, bf16[512,768]{1,0:T(8,128)(2,1)}, u32[]{:S(2)}, u32[]{:S(2)}) collective-permute-start(bf16[512,768]{1,0:T(8,128)(2,1)} %get-tuple-element.119), channel_id=1, source_target_pairs={{0,1},{1,0},{2,3},{3,2},{4,5},{5,4},{6,7},{7,6},{8,9},{9,8},{10,11... | collective-permute-start | bytes 2359304 | tf_op jit(solution)/shard_map/ppermute | solution.py:394
  154.5 53.7 %collective-permute-start.13 = (bf16[1536,768]{1,0:T(8,128)(2,1)}, bf16[1536,768]{1,0:T(8,128)(2,1)}, u32[]{:S(2)}, u32[]{:S(2)}) collective-permute-start(bf16[1536,768]{1,0:T(8,128)(2,1)} %fusion.11), channel_id=1, source_target_pairs={{0,1},{1,0},{2,3},{3,2},{4,5},{5,4},{6,7},{7,6},{8,9},{9,8},{10,11... | collective-permute-start | bytes 7077896 | tf_op jit(solution)/shard_map/ppermute | solution.py:522
  256.3 37.8 %collective-permute-start.30 = (bf16[2,192,1792]{2,1,0:T(8,128)(2,1)}, bf16[2,192,1792]{2,1,0:T(8,128)(2,1)}, u32[]{:S(2)}, u32[]{:S(2)}) collective-permute-start(bf16[2,192,1792]{2,1,0:T(8,128)(2,1)} %dynamic-slice_convert_fusion.1), channel_id=1, source_target_pairs={{0,2},{2,0},{4,6},{6,4},{8,10},{10,8},{12,14},{14,12},{16,18},{18,... | collective-permute-start | bytes 4128776 | tf_op jit(solution)/shard_map/ppermute | solution.py:404
  288.5 14.3 %collective-permute-start.20 = (bf16[1,768,768]{2,1,0:T(8,128)(2,1)S(1)}, bf16[1,768,768]{2,1,0:T(8,128)(2,1)S(1)}, u32[]{:S(2)}, u32[]{:S(2)}) collective-permute-start(bf16[1,768,768]{2,1,0:T(8,128)(2,1)S(1)} %copy-done.24), channel_id=1, source_target_pairs={{0,2},{2,0},{4,6},{6,4},{8,10},{10,8},{12,14},{14,12},{16,18},{18,... | collective-permute-start | bytes 3538952 | tf_op jit(solution)/shard_map/ppermute | solution.py:404
  296.7 16.8 %collective-permute-start.31 = (bf16[192,1792]{1,0:T(8,128)(2,1)S(1)}, bf16[192,1792]{1,0:T(8,128)(2,1)S(1)}, u32[]{:S(2)}, u32[]{:S(2)}) collective-permute-start(bf16[192,1792]{1,0:T(8,128)(2,1)S(1)} %fusion.14), channel_id=1, source_target_pairs={{0,1},{1,0},{2,3},{3,2},{4,5},{5,4},{6,7},{7,6},{8,9},{9,8},{10,11... | collective-permute-start | bytes 2064392 | tf_op jit(solution)/shard_map/ppermute | solution.py:544
  300.2 15.9 %collective-permute-start.19 = (f32[14884]{0:T(1024)S(1)}, f32[14884]{0:T(1024)S(1)}, u32[]{:S(2)}, u32[]{:S(2)}) collective-permute-start(f32[14884]{0:T(1024)S(1)} %add.195), channel_id=1, source_target_pairs={{0,16},{2,18},{4,20},{6,22},{8,24},{10,26},{12,28},{14,30},{16,0},... | collective-permute-start | bytes 178616 | tf_op jit(solution)/shard_map/ppermute | solution.py:404
  304.1 18.0 %collective-permute-start.21 = (bf16[384,768]{1,0:T(8,128)(2,1)}, bf16[384,768]{1,0:T(8,128)(2,1)}, u32[]{:S(2)}, u32[]{:S(2)}) collective-permute-start(bf16[384,768]{1,0:T(8,128)(2,1)} %fusion.15), channel_id=1, source_target_pairs={{0,4},{2,6},{4,0},{6,2},{8,12},{10,14},{12,8},{14,10},{16,20},{18,... | collective-permute-start | bytes 1769480 | tf_op jit(solution)/shard_map/ppermute | solution.py:444
  315.1 69.2 %collective-permute-start.14 = (bf16[512,768]{1,0:T(8,128)(2,1)S(1)}, bf16[512,768]{1,0:T(8,128)(2,1)}, u32[]{:S(2)}, u32[]{:S(2)}) collective-permute-start(bf16[512,768]{1,0:T(8,128)(2,1)S(1)} %get-tuple-element.117), channel_id=1, source_target_pairs={{0,1},{1,0},{2,3},{3,2},{4,5},{5,4},{6,7},{7,6},{8,9},{9,8},{10,11... | collective-permute-start | bytes 2359304 | tf_op jit(solution)/shard_map/ppermute | solution.py:394
  326.3 16.8 %collective-permute-start.34 = (bf16[24,1792]{1,0:T(8,128)(2,1)S(1)}, bf16[24,1792]{1,0:T(8,128)(2,1)S(1)}, u32[]{:S(2)}, u32[]{:S(2)}) collective-permute-start(bf16[24,1792]{1,0:T(8,128)(2,1)S(1)} %get-tuple-element.137), channel_id=1, source_target_pairs={{0,16},{2,18},{4,20},{6,22},{8,24},{10,26},{12,28},{14,30},{16,0},... | collective-permute-start | bytes 258056 | tf_op jit(solution)/shard_map/ppermute | solution.py:444
  327.8 15.3 %collective-permute-start.33 = (bf16[24,1792]{1,0:T(8,128)(2,1)S(1)}, bf16[24,1792]{1,0:T(8,128)(2,1)S(1)}, u32[]{:S(2)}, u32[]{:S(2)}) collective-permute-start(bf16[24,1792]{1,0:T(8,128)(2,1)S(1)} %get-tuple-element.135), channel_id=1, source_target_pairs={{0,8},{2,10},{4,12},{6,14},{8,0},{10,2},{12,4},{14,6},{16,24},{18,... | collective-permute-start | bytes 258056 | tf_op jit(solution)/shard_map/ppermute | solution.py:444
  330.4 12.9 %collective-permute-start.24 = (bf16[96,768]{1,0:T(8,128)(2,1)S(1)}, bf16[96,768]{1,0:T(8,128)(2,1)S(1)}, u32[]{:S(2)}, u32[]{:S(2)}) collective-permute-start(bf16[96,768]{1,0:T(8,128)(2,1)S(1)} %get-tuple-element.127), channel_id=1, source_target_pairs={{0,24},{2,26},{4,28},{6,30},{8,16},{10,18},{12,20},{14,22},{16,8},... | collective-permute-start | bytes 442376 | tf_op jit(solution)/shard_map/ppermute | solution.py:444
  332.6 21.8 %collective-permute-start.23 = (bf16[96,768]{1,0:T(8,128)(2,1)S(1)}, bf16[96,768]{1,0:T(8,128)(2,1)S(1)}, u32[]{:S(2)}, u32[]{:S(2)}) collective-permute-start(bf16[96,768]{1,0:T(8,128)(2,1)S(1)} %get-tuple-element.128), channel_id=1, source_target_pairs={{0,16},{2,18},{4,20},{6,22},{8,24},{10,26},{12,28},{14,30},{16,0},... | collective-permute-start | bytes 442376 | tf_op jit(solution)/shard_map/ppermute | solution.py:444
  343.1 11.3 %collective-permute-start.22 = (bf16[96,768]{1,0:T(8,128)(2,1)S(1)}, bf16[96,768]{1,0:T(8,128)(2,1)S(1)}, u32[]{:S(2)}, u32[]{:S(2)}) collective-permute-start(bf16[96,768]{1,0:T(8,128)(2,1)S(1)} %get-tuple-element.126), channel_id=1, source_target_pairs={{0,8},{2,10},{4,12},{6,14},{8,0},{10,2},{12,4},{14,6},{16,24},{18,... | collective-permute-start | bytes 442376 | tf_op jit(solution)/shard_map/ppermute | solution.py:444
  343.2 11.4 %collective-permute-start.36 = (bf16[24,1792]{1,0:T(8,128)(2,1)S(1)}, bf16[24,1792]{1,0:T(8,128)(2,1)S(1)}, u32[]{:S(2)}, u32[]{:S(2)}) collective-permute-start(bf16[24,1792]{1,0:T(8,128)(2,1)S(1)} %add_convert_fusion.2), channel_id=1, source_target_pairs={{0,24},{2,26},{4,28},{6,30},{8,16},{10,18},{12,20},{14,22},{16,8},... | collective-permute-start | bytes 258056 | tf_op jit(solution)/shard_map/ppermute | solution.py:444
  343.3 15.9 %collective-permute-start.37 = (bf16[24,1792]{1,0:T(8,128)(2,1)S(1)}, bf16[24,1792]{1,0:T(8,128)(2,1)S(1)}, u32[]{:S(2)}, u32[]{:S(2)}) collective-permute-start(bf16[24,1792]{1,0:T(8,128)(2,1)S(1)} %add_convert_fusion.2), channel_id=1, source_target_pairs={{0,16},{2,18},{4,20},{6,22},{8,24},{10,26},{12,28},{14,30},{16,0},... | collective-permute-start | bytes 258056 | tf_op jit(solution)/shard_map/ppermute | solution.py:444
  354.6 12.1 %collective-permute-start.26 = (bf16[96,768]{1,0:T(8,128)(2,1)S(1)}, bf16[96,768]{1,0:T(8,128)(2,1)S(1)}, u32[]{:S(2)}, u32[]{:S(2)}) collective-permute-start(bf16[96,768]{1,0:T(8,128)(2,1)S(1)} %add_convert_fusion.1), channel_id=1, source_target_pairs={{0,16},{2,18},{4,20},{6,22},{8,24},{10,26},{12,28},{14,30},{16,0},... | collective-permute-start | bytes 442376 | tf_op jit(solution)/shard_map/ppermute | solution.py:444
  366.9 16.4 %collective-permute-start.28 = (bf16[384,768]{1,0:T(8,128)(2,1)S(1)}, bf16[384,768]{1,0:T(8,128)(2,1)S(1)}, u32[]{:S(2)}, u32[]{:S(2)}) collective-permute-start(bf16[384,768]{1,0:T(8,128)(2,1)S(1)} %pad_maximum_fusion.16), channel_id=1, source_target_pairs={{0,4},{2,6},{4,0},{6,2},{8,12},{10,14},{12,8},{14,10},{16,20},{18,... | collective-permute-start | bytes 1769480 | tf_op jit(solution)/shard_map/ppermute | solution.py:444
  373.3 13.8 %collective-permute-start.40 = (bf16[192,1792]{1,0:T(8,128)(2,1)S(1)}, bf16[192,1792]{1,0:T(8,128)(2,1)S(1)}, u32[]{:S(2)}, u32[]{:S(2)}) collective-permute-start(bf16[192,1792]{1,0:T(8,128)(2,1)S(1)} %pad_maximum_fusion.13), channel_id=1, source_target_pairs={{0,2},{2,0},{4,6},{6,4},{8,10},{10,8},{12,14},{14,12},{16,18},{18,... | collective-permute-start | bytes 2064392 | tf_op jit(solution)/shard_map/ppermute | solution.py:404
  (51 other events, 376.4 us)
